TPU v7x, 256 devices: a whole 4x4x8 slice. The times are simulated.
256 devices in a mesh: slab: 16 (over z, x_hi), flow: 16 (over y, x_lo, core).
Axes of the slice: x: 4 (x_hi: 2, x_lo: 2; x = x_hi * 2 + x_lo), y: 4, z: 8, core: 2. Of those that a mesh axis runs over, the one named last changes fastest.
Arguments:
- populations: float32 [19, 128, 512, 256], P(None, 'slab', 'flow'), as said below
- offsets: int32 [2], replicated, may hold values from 0 to 511
- fraction: int32 [2], replicated, may hold values from 0 to 63
Outputs:
- advanced: float32 [19, 128, 512, 256], P(None, 'slab', 'flow')
- tallies: float32 [2, 4], replicated
Inputs may be any that keep to these rules, and one draw needn't show every extreme that they name: `populations`: every entry is positive.
All inputs are finite; a program needn't handle non-finite values.
Results may differ from a plain program's by a relative error of at most 0.0001.
Values sent between devices are 32-bit elements; how exact they have to be, the bound alone decides.
No kernel may reach another device: no remote copies, remote signals or barrier semaphores. Data moves between devices by JAX's collectives and lax.ppermute only.
A program may use at most 128 MiB of HBM per device.

v0:
```python
import jax
import jax.numpy as jnp
from jax import lax
from jax.experimental import pallas as pl
from jax.experimental.pallas import tpu as pltpu
from jax.sharding import PartitionSpec as P

STEPS = 2
DEN = 64

VELOCITY = (
    (0, 0, 0),
    (1, 0, 0),
    (-1, 0, 0),
    (0, 1, 0),
    (0, -1, 0),
    (0, 0, 1),
    (0, 0, -1),
    (1, 1, 0),
    (-1, -1, 0),
    (1, -1, 0),
    (-1, 1, 0),
    (1, 0, 1),
    (-1, 0, -1),
    (1, 0, -1),
    (-1, 0, 1),
    (0, 1, 1),
    (0, -1, -1),
    (0, 1, -1),
    (0, -1, 1),
)
WEIGHTS = (1.0 / 3.0,) + (1.0 / 18.0,) * 6 + (1.0 / 36.0,) * 12
OMEGA = 1.0 / 1.4
SLIDE = 0.1
LEVEL = (0, 1, 2, 5, 6, 11, 12, 13, 14)
UPWARD = (3, 7, 10, 15, 17)
DOWNWARD = (4, 8, 9, 16, 18)
RIGHTWARD = (1, 7, 9, 11, 13)
LEFTWARD = (2, 8, 10, 12, 14)
EDGES = UPWARD + DOWNWARD
REACH = 16
HALO = 10 * REACH
EXTRA = HALO + 40
ROWS = EXTRA + 8


def moments(f):
    diff = [None] + [f[2 * k - 1] - f[2 * k] for k in range(1, 10)]
    rho = f[0]
    for k in range(1, 10):
        rho = rho + (f[2 * k - 1] + f[2 * k])
    m_x = (diff[1] + diff[4]) + (diff[5] + diff[6]) + diff[7]
    m_y = (diff[2] + diff[4]) - (diff[5] - diff[8]) + diff[9]
    m_z = (diff[3] + diff[6]) - (diff[7] - diff[8]) - diff[9]
    return rho, m_x, m_y, m_z


def along(n, u_x, u_y, u_z):
    total = None
    for c, u in zip(VELOCITY[n], (u_x, u_y, u_z)):
        if c:
            term = u if c > 0 else -u
            total = term if total is None else total + term
    return total


def collide(f, rho, m_x, m_y, m_z):
    inverse = 1.0 / rho
    u_x, u_y, u_z = m_x * inverse, m_y * inverse, m_z * inverse
    base = 1.0 - 1.5 * (u_x * u_x + u_y * u_y + u_z * u_z)
    post = [(1.0 - OMEGA) * f[0] + (WEIGHTS[0] * OMEGA) * rho * base]
    for n in range(1, 19, 2):
        scale = (WEIGHTS[n] * OMEGA) * rho
        c_u = along(n, u_x, u_y, u_z)
        even = scale * (base + 4.5 * (c_u * c_u))
        odd = (3.0 * scale) * c_u
        post.append((1.0 - OMEGA) * f[n] + (even + odd))
        post.append((1.0 - OMEGA) * f[n + 1] + (even - odd))
    return post, u_x, u_y, u_z


def wall_change(n, rho, u_x, u_y, u_z, slide):
    c_x = VELOCITY[n][0]
    terms = -3.0 * slide * u_x - 1.5 * slide * slide
    if c_x:
        terms = terms + (
            3.0 * slide * c_x + 4.5 * slide * slide + (9.0 * slide * c_x) * along(n, u_x, u_y, u_z)
        )
    return (WEIGHTS[n] * rho) * terms


def roll_lanes(v, shift):
    return pltpu.roll(v, shift % v.shape[1], axis=1) if shift else v


def sum_of(values):
    total = values[0]
    for value in values[1:]:
        total = total + value
    return total


def store_edges(load, p_ref, y, side, e_ref, mr_ref, ml_ref, acc_ref):
    members, slide = ((UPWARD, -SLIDE), (DOWNWARD, SLIDE))[side]
    cells = e_ref.shape[1]
    for lo in range(0, cells, 8):
        rows = slice(lo, lo + 8)
        rho, m_x, m_y, m_z = moments(load(y, lo))
        inverse = 1.0 / rho
        u_x, u_y, u_z = m_x * inverse, m_y * inverse, m_z * inverse
        values = []
        for k, n in enumerate(members):
            j = 5 * side + k
            value = p_ref[n, y, rows, :] + wall_change(n, rho, u_x, u_y, u_z, slide)
            values.append(value)
            e_ref[j, rows, :] = value
            if lo < REACH:
                ml_ref[j * REACH + lo : j * REACH + lo + 8, :] = value
            if lo >= cells - REACH:
                at = j * REACH + lo - (cells - REACH)
                mr_ref[at : at + 8, :] = value
            if VELOCITY[n][0] == 1 and lo == cells - REACH - 8:
                mr_ref[EXTRA + side : EXTRA + side + 1, :] = value[7:8]
            if VELOCITY[n][0] == -1 and lo == REACH:
                ml_ref[EXTRA + side : EXTRA + side + 1, :] = value[0:1]
        if acc_ref is not None:
            acc_ref[5] += (slide / 3.0) * sum_of(values)


def collide_row(y, load, p_ref, mr_ref, ml_ref, acc_ref, slab_rows):
    cells = p_ref.shape[2]
    for lo in range(0, cells, 8):
        rows = slice(lo, lo + 8)
        f = load(y, lo)
        rho, m_x, m_y, m_z = moments(f)
        post = collide(f, rho, m_x, m_y, m_z)[0]
        for n in range(19):
            p_ref[n, y, rows, :] = post[n]
        if acc_ref is not None:
            acc_ref[0] += rho
            acc_ref[1] += m_x
            acc_ref[2] += m_y
            acc_ref[3] += m_z
            top, bottom = y == slab_rows - 1, y == 0
            edge = jnp.where(bottom, SLIDE, 0.0) - jnp.where(top, SLIDE, 0.0)
            both = jnp.where(bottom | top, SLIDE, 0.0)
            acc_ref[4] += (edge / 6.0) * rho - (both / 2.0) * m_y
            level, up, down = (sum_of([post[n] for n in ns]) for ns in (LEVEL, UPWARD, DOWNWARD))
            below_top = jnp.where(y == slab_rows - 2, -SLIDE * 2.0 / 3.0, 0.0)
            above_bottom = jnp.where(y == 1, SLIDE * 2.0 / 3.0, 0.0)
            acc_ref[5] += (edge / 6.0) * level + (below_top * up + above_bottom * down)
    for k, n in enumerate(RIGHTWARD):
        mr_ref[pl.ds(HALO + 8 * k + y, 1), :] = p_ref[n, y, cells - 1 : cells, :]
    for k, n in enumerate(LEFTWARD):
        ml_ref[pl.ds(HALO + 8 * k + y, 1), :] = p_ref[n, y, 0:1, :]


def clear_rest(*messages):
    for message in messages:
        message[EXTRA:ROWS, :] = jnp.zeros((ROWS - EXTRA, message.shape[1]), jnp.float32)


def first_kernel(f_hbm, p_hbm, e_ref, mr_ref, ml_ref, t_ref, f_ref, p_ref, acc_ref, in_sems, out_sems):
    slab_rows = f_ref.shape[1]

    def arriving(y):
        return pltpu.make_async_copy(f_hbm.at[:, y], f_ref.at[:, y], in_sems.at[y])

    def leaving(y):
        return pltpu.make_async_copy(p_ref.at[:, y], p_hbm.at[:, y], out_sems.at[y])

    for y in range(slab_rows):
        arriving(y).start()
    acc_ref[...] = jnp.zeros_like(acc_ref)
    clear_rest(mr_ref, ml_ref)

    def load(y, lo):
        return [f_ref[n, y, lo : lo + 8, :] for n in range(19)]

    def step(y, carry):
        arriving(y).wait()
        collide_row(y, load, p_ref, mr_ref, ml_ref, acc_ref, slab_rows)
        leaving(y).start()
        return carry

    lax.fori_loop(0, slab_rows, step, 0)
    store_edges(load, p_ref, slab_rows - 1, 0, e_ref, mr_ref, ml_ref, acc_ref)
    store_edges(load, p_ref, 0, 1, e_ref, mr_ref, ml_ref, acc_ref)
    lane = lax.broadcasted_iota(jnp.int32, t_ref.shape, 2)
    out = jnp.zeros(t_ref.shape, jnp.float32)
    for q in range(6):
        out = out + jnp.where(lane == q, jnp.sum(acc_ref[q]), 0.0)
    t_ref[...] = out
    for y in range(slab_rows):
        leaving(y).wait()


def streamed(p_ref, rl, rr, wu, wd, slab_rows):
    cells = p_ref.shape[2]
    row = lax.broadcasted_iota(jnp.int32, (8, p_ref.shape[3]), 0)

    def load(y, lo):
        out = []
        for n, (c_x, c_y, c_z) in enumerate(VELOCITY):
            if c_y == 1 and isinstance(y, int) and y == 0:
                v = wu[UPWARD.index(n), lo : lo + 8, :]
            elif c_y == -1 and isinstance(y, int) and y == slab_rows - 1:
                v = wd[DOWNWARD.index(n), lo : lo + 8, :]
            elif c_x == 1 and lo == 0:
                halo = rl[pl.ds(HALO + 8 * RIGHTWARD.index(n) + y - c_y, 1), :]
                v = jnp.where(row == 0, halo, pltpu.roll(p_ref[n, y - c_y, 0:8, :], 1, axis=0))
            elif c_x == -1 and lo == cells - 8:
                halo = rr[pl.ds(HALO + 8 * LEFTWARD.index(n) + y - c_y, 1), :]
                v = jnp.where(
                    row == 7, halo, pltpu.roll(p_ref[n, y - c_y, cells - 8 : cells, :], 7, axis=0)
                )
            else:
                v = p_ref[n, y - c_y, lo - c_x : lo - c_x + 8, :]
            out.append(roll_lanes(v, c_z))
        return out

    return load


def next_kernel(
    all_cells,
    step_ref,
    p_hbm,
    rl,
    rr,
    wu,
    wd,
    g_ref,
    o_hbm,
    e_ref,
    mr_ref,
    ml_ref,
    s_ref,
    p_ref,
    q_ref,
    in_sems,
    out_sems,
):
    slab_rows, cells = p_ref.shape[1:3]

    def arriving(y):
        return pltpu.make_async_copy(p_hbm.at[:, y], p_ref.at[:, y], in_sems.at[y])

    def leaving(y):
        return pltpu.make_async_copy(q_ref.at[:, y], o_hbm.at[:, y], out_sems.at[y])

    for y in range(slab_rows):
        arriving(y).start()
    clear_rest(mr_ref, ml_ref)
    total = g_ref[0] * (1.0 / all_cells)
    lane = lax.broadcasted_iota(jnp.int32, total.shape, 1)
    rho, m_x, m_y, m_z, first, second = (
        jnp.sum(jnp.where(lane == q, total, 0.0)) for q in range(6)
    )
    at = lax.broadcasted_iota(jnp.int32, s_ref.shape, 1)
    x = m_x + first + jnp.where(lax.broadcasted_iota(jnp.int32, s_ref.shape, 0) == 1, second, 0.0)
    s_ref[...] = jnp.where(at == 0, rho, jnp.where(at == 1, x, jnp.where(at == 2, m_y, m_z)))

    load = streamed(p_ref, rl, rr, wu, wd, slab_rows)

    def all_rows(work):
        def step(y, carry):
            arriving(y + 1).wait()
            work(y)
            leaving(y).start()
            return carry

        arriving(0).wait()
        step(0, 0)
        lax.fori_loop(1, slab_rows - 1, step, 0)
        work(slab_rows - 1)
        leaving(slab_rows - 1).start()

    def store(y):
        for lo in range(0, cells, 8):
            for n, v in enumerate(load(y, lo)):
                q_ref[n, y, lo : lo + 8, :] = v

    @pl.when(step_ref[0] < STEPS - 1)
    def _():
        all_rows(lambda y: collide_row(y, load, q_ref, mr_ref, ml_ref, None, slab_rows))
        store_edges(load, q_ref, slab_rows - 1, 0, e_ref, mr_ref, ml_ref, None)
        store_edges(load, q_ref, 0, 1, e_ref, mr_ref, ml_ref, None)

    @pl.when(step_ref[0] == STEPS - 1)
    def _():
        all_rows(store)

    for y in range(slab_rows):
        leaving(y).wait()


def wall_kernel(step_ref, d_ref, n_ref, g_ref, e_ref, rl, rr, up_ref, down_ref, t_ref, s_ref):
    cells = e_ref.shape[1]
    own = REACH + 8
    section = step_ref[0]
    r = lax.rem(d_ref[section] + REACH, cells) - REACH
    a = n_ref[section].astype(jnp.float32) * (1.0 / DEN)
    t_ref[...] = jnp.broadcast_to(jnp.sum(g_ref[...], axis=0, keepdims=True), t_ref.shape)
    for j, n in enumerate(EDGES):
        side, c_x = j // 5, VELOCITY[n][0]
        s_ref[8:own, :] = rl[j * REACH : (j + 1) * REACH, :]
        s_ref[own : own + cells, :] = e_ref[j]
        s_ref[own + cells : own + cells + REACH, :] = rr[j * REACH : (j + 1) * REACH, :]
        if c_x == 1:
            s_ref[7:8, :] = rl[EXTRA + side : EXTRA + side + 1, :]
        if c_x == -1:
            s_ref[own + cells + REACH : own + cells + REACH + 1, :] = rr[
                EXTRA + side : EXTRA + side + 1, :
            ]
        if side == 0:
            start, out = own - c_x + r, up_ref
            low, high = 1.0 - a, a
        else:
            start, out = own - c_x - r - 1, down_ref
            low, high = a, 1.0 - a
        line = s_ref[...]
        count = line.shape[0]
        line = low * line + high * pltpu.roll(line, count - 1, axis=0)
        out[j % 5] = pltpu.roll(line, count - start, axis=0)[:cells]


VMEM = pl.BlockSpec(memory_space=pltpu.VMEM)
SMEM = pl.BlockSpec(memory_space=pltpu.SMEM)
HBM = pl.BlockSpec(memory_space=pltpu.HBM)
PARAMS = pltpu.CompilerParams(vmem_limit_bytes=24 * 1024 * 1024)


def near(*shape):
    return pltpu.VMEM(shape, jnp.float32)


def kept(*values):
    return tuple(pltpu.with_memory_space_constraint(v, pltpu.VMEM) for v in values)


def local(populations, offsets, fraction):
    _, slab_rows, cells, depth = shape = populations.shape
    slabs, flows = lax.axis_size("slab"), lax.axis_size("flow")
    all_cells = slab_rows * cells * depth * slabs * flows
    side = (5, cells, depth)
    both = ("slab", "flow")
    everyone = [(s, f) for s in range(slabs) for f in range(flows)]

    def beside(value, distance):
        route = [((i - distance) % flows, i) for i in range(flows)]
        return lax.ppermute(value, "flow", route)

    def displaced(value, slab_step, flow_step):
        route = [
            (((s + slab_step) % slabs) * flows + (f + flow_step) % flows, s * flows + f)
            for s, f in everyone
        ]
        return lax.ppermute(value, both, route)

    state = pltpu.HBM(shape, jnp.float32)
    edge_outs = (
        near(10, cells, depth),
        near(ROWS, depth),
        near(ROWS, depth),
    )
    buffers = [pltpu.VMEM(shape, jnp.float32)] * 2
    row_sems = [pltpu.SemaphoreType.DMA((slab_rows,))] * 2

    first = pl.pallas_call(
        first_kernel,
        out_shape=(state,) + edge_outs + (near(flows, 1, 128),),
        in_specs=[HBM],
        out_specs=(HBM,) + (VMEM,) * 4,
        scratch_shapes=buffers + [pltpu.VMEM((6, 8, depth), jnp.float32)] + row_sems,
        compiler_params=PARAMS,
        name="first",
    )
    walls = pl.pallas_call(
        wall_kernel,
        out_shape=(near(*side), near(*side), near(slabs, 1, 128)),
        in_specs=[SMEM] * 3 + [VMEM] * 4,
        out_specs=(VMEM,) * 3,
        scratch_shapes=[pltpu.VMEM((cells + 2 * REACH + 16, depth), jnp.float32)],
        compiler_params=PARAMS,
        name="walls",
    )
    following = pl.pallas_call(
        lambda *refs: next_kernel(all_cells, *refs),
        out_shape=(state,) + edge_outs + (near(STEPS, 4),),
        in_specs=[SMEM, HBM] + [VMEM] * 5,
        out_specs=(HBM,) + (VMEM,) * 4,
        scratch_shapes=buffers + row_sems,
        input_output_aliases={1: 0},
        compiler_params=PARAMS,
        name="following",
    )

    def leaf(blocks_apart):
        return lambda up, down: (
            displaced(up, -1, blocks_apart),
            displaced(down, 1, -blocks_apart),
        )

    def twig(start, count):
        leaves = [leaf(start + k) for k in range(count)]
        return lambda inner, up, down: lax.switch(inner, leaves, up, down)

    count = 4
    branches = [twig(start, count) for start in range(0, flows, count)]
    blocks = [((offsets[k] + REACH) // cells) % flows for k in range(STEPS)]

    def neighbours(axis, mr, ml, sums):
        from_left, from_right = beside(mr, 1), beside(ml, -1)
        return from_left, from_right, lax.all_to_all(sums, axis, 0, 0)

    def step(section, carry):
        p, edges, from_left, from_right, gathered, _, now, *later = carry
        at = section.reshape(1)
        up, down, sums = walls(
            at, offsets, fraction, *kept(gathered, edges, from_left, from_right)
        )
        wu, wd = lax.switch(now // count, branches, now % count, up, down)
        p, edges, mr, ml, totals = following(
            at,
            pltpu.with_memory_space_constraint(p, pltpu.HBM),
            *kept(from_left, from_right, wu, wd, sums),
        )
        from_left, from_right, gathered = lax.cond(
            section < STEPS - 1,
            lambda mr, ml, sums: neighbours("slab", mr, ml, sums),
            lambda mr, ml, sums: (mr, ml, sums),
            mr,
            ml,
            sums,
        )
        return p, edges, from_left, from_right, gathered, totals, *later, now

    p, edges, mr, ml, sums = first(pltpu.with_memory_space_constraint(populations, pltpu.HBM))
    from_left, from_right, gathered = neighbours("flow", mr, ml, sums)
    totals = jnp.zeros((STEPS, 4), jnp.float32)
    carry = (p, edges, from_left, from_right, gathered, totals, *blocks)
    carry = lax.fori_loop(0, STEPS, step, carry)
    return carry[0], carry[5]


def solution(mesh):
    in_specs = (P(None, "slab", "flow", None), P(), P())
    out_specs = (P(None, "slab", "flow", None), P())
    return jax.shard_map(local, mesh=mesh, in_specs=in_specs, out_specs=out_specs, check_vma=False)
```

profile of v0, /device:TPU:4, one launch (start us, length us, event | category | flops | bytes accessed | tf_op | source)
XLA Modules:
  0.0 78.4 jit_solution(7603100852448507502)
XLA Ops:
  0.6 4.7 %first.1 = (f32[19,8,32,256]{3,2,1,0:T(8,128)}, f32[10,32,256]{2,1,0:T(8,128)S(1)}, f32[208,256]{1,0:T(8,128)S(1)}, f32[208,256]{1,0:T(8,128)S(1)}, f32[16,1,128]{2,1,0:T(1,128)}) custom-call(f32[19,8,32,256]{3,2,1,0:T(8,128)} %f_hbm.1), custom_call_target="tpu_custom_call" | custom-call | tf_op jit(solution)/shard_map/first/pallas_call | solution.py:439
  5.5 3.8 %collective-permute-start.35 = (f32[208,256]{1,0:T(8,128)S(1)}, f32[208,256]{1,0:T(8,128)S(1)}, u32[]{:S(2)}, u32[]{:S(2)}) collective-permute-start(f32[208,256]{1,0:T(8,128)S(1)} %get-tuple-element.441), channel_id=1, source_target_pairs={{1,0},{2,1},{3,2},{4,3},{5,4},{6,5},{7,6},{8,7},{9,8},{10,9},{11,1... | collective-permute-start | bytes 638984 | tf_op jit(solution)/shard_map/ppermute | solution.py:352
  9.3 3.4 %all-to-all-start.1 = ((f32[16,1,128]{2,1,0:T(1,128)}), f32[16,1,128]{2,1,0:T(1,128)S(1)}, u32[]{:S(2)}, u32[]{:S(2)}) async-start(f32[16,1,128]{2,1,0:T(1,128)} %get-tuple-element.442), calls=%async_computation.1 | async-start | bytes 16384 | tf_op jit(solution)/shard_map/all_to_all | solution.py:415
  12.7 0.6 fusion
  14.7 4.0 %all-to-all-done.1 = f32[16,1,128]{2,1,0:T(1,128)S(1)} async-done(((f32[16,1,128]{2,1,0:T(1,128)}), f32[16,1,128]{2,1,0:T(1,128)S(1)}, u32[]{:S(2)}, u32[]{:S(2)}) %all-to-all-start.1) | async-done | bytes 8224 | tf_op jit(solution)/shard_map/all_to_all | solution.py:415
  18.7 59.1 %while.29 = (s32[]{:T(128)}, f32[19,8,32,256]{3,2,1,0:T(8,128)}, f32[10,32,256]{2,1,0:T(8,128)S(1)}, f32[208,256]{1,0:T(8,128)S(1)}, f32[208,256]{1,0:T(8,128)S(...) while((s32[]{:T(128)}, f32[19,8,32,256]{3,2,1,0:T(8,128)}, ...), condition=%wide.region_23.24_spmd, body=%wide.region_0.23_spmd.sunk | while | flops 25 | bytes 4768446 | solution.py:443
  19.0 0.8 %walls.8 = (f32[5,32,256]{2,1,0:T(8,128)S(1)}, f32[5,32,256]{2,1,0:T(8,128)S(1)}, f32[16,1,128]{2,1,0:T(1,128)S(1)}) custom-call(s32[1]{0:T(128)} %bitcast.4.step_ref.refs_0_, s32[2]{0:T(128)S(1)} %get-tuple-element.649.d_ref, s32[2]{0:T(128)S(1)} %get-tuple-element.650.n_ref, f32[16,1,128]{2,1,0:T(1,128)S(1)} %get-tuple-element.628.g_ref, ...), custom_call_target="tpu_custom_call" | custom-call | tf_op jit(solution)/shard_map/while/body/eval_jaxpr/walls/pallas_call | solution.py:420
  19.8 12.1 %conditional.8 = ((f32[5,32,256]{2,1,0:T(8,128)}, f32[5,32,256]{2,1,0:T(8,128)})) conditional(s32[]{:T(128)} %clamp.23, (s32[]{:T(128)}, f32[5,32,256]{2,1,0:T(8,128)S(1)}, f32[5,32,256]{2,1,0:T(8,128)S(1)}) %tuple.126, (s32[]{:T(128)}, f32[5,32,256]{2,1,0:T(8,128)S(1)}, f32[5,32,256]{2,1,0:T(8,128)S(1)}) %tuple.126, ...), branch_computations={%region_1.5_spmd, %region_6.10_spmd, %region_11.15_spmd, %region_1... | conditional | flops 1 | bytes 1310856 | solution.py:423
  19.8 12.1 %conditional = (f32[5,32,256]{2,1,0:T(8,128)}, f32[5,32,256]{2,1,0:T(8,128)}) conditional(s32[]{:T(128)} %clamp.17, (f32[5,32,256]{2,1,0:T(8,128)S(1)}, f32[5,32,256]{2,1,0:T(8,128)S(1)}) %tuple.74, (f32[5,32,256]{2,1,0:T(8,128)S(1)}, f32[5,32,256]{2,1,0:T(8,128)S(1)}) %tuple.74, (f32[5,32,256]{2,1,0:T(8,128)S(1)}, ...), branch_computations={%region_2.1_spmd, %region_3.2_spmd, %region_4.3_spmd, %region_5.4_... | conditional | bytes 1310816 | solution.py:407
  19.8 2.0 %collective-permute-start.6 = (f32[5,32,256]{2,1,0:T(8,128)S(1)}, f32[5,32,256]{2,1,0:T(8,128)}, u32[]{:S(2)}, u32[]{:S(2)}) collective-permute-start(f32[5,32,256]{2,1,0:T(8,128)S(1)} %get-tuple-element.364), channel_id=1, source_target_pairs={{243,0},{244,1},{245,2},{246,3},{247,4},{248,5},{249,6},{250,7},{2... | collective-permute-start | bytes 491528 | tf_op jit(solution)/shard_map/while/body/eval_jaxpr/cond/branch_0_fun/cond/branch_3_fun/ppermute | solution.py:359
  21.9 3.7 %collective-permute-done.6 = f32[5,32,256]{2,1,0:T(8,128)} collective-permute-done((f32[5,32,256]{2,1,0:T(8,128)S(1)}, f32[5,32,256]{2,1,0:T(8,128)}, u32[]{:S(2)}, u32[]{:S(2)}) %collective-permute-start.6) | collective-permute-done | bytes 163872 | tf_op jit(solution)/shard_map/while/body/eval_jaxpr/cond/branch_0_fun/cond/branch_3_fun/ppermute | solution.py:359
  25.5 6.4 %collective-permute-done.7 = f32[5,32,256]{2,1,0:T(8,128)} collective-permute-done((f32[5,32,256]{2,1,0:T(8,128)S(1)}, f32[5,32,256]{2,1,0:T(8,128)}, u32[]{:S(2)}, u32[]{:S(2)}) %collective-permute-start.7) | collective-permute-done | bytes 163872 | tf_op jit(solution)/shard_map/while/body/eval_jaxpr/cond/branch_0_fun/cond/branch_3_fun/ppermute | solution.py:359
  31.9 6.4 %following.8 = (f32[19,8,32,256]{3,2,1,0:T(8,128)}, f32[10,32,256]{2,1,0:T(8,128)S(1)}, f32[208,256]{1,0:T(8,128)S(1)}, f32[208,256]{1,0:T(8,128)S(1)}, f32[2,4]{1,0:T(2,128)S(1)}) custom-call(s32[1]{0:T(128)} %bitcast.4.step_ref.refs_0_, f32[19,8,32,256]{3,2,1,0:T(8,128)} %get-tuple-element.624.refs_1_, ...), custom_call_target="tpu_custom_call", output_to_operand_aliasing={{0}: (1, {})} | custom-call | tf_op jit(solution)/shard_map/while/body/eval_jaxpr/following/pallas_call | solution.py:424
  38.3 22.2 %conditional.9 = ((f32[208,256]{1,0:T(8,128)S(1)}, f32[208,256]{1,0:T(8,128)S(1)}, f32[16,1,128]{2,1,0:T(1,128)S(1)})) conditional(s32[]{:T(128)} %convert_element_type.11, (f32[208,256]{1,0:T(8,128)S(1)}, f32[208,256]{1,0:T(8,128)S(1)}, f32[16,1,128]{2,1,0:T(1,128)S(1)}) %tuple.127, (f32[208,256]{1,0:T(8,128)S(1)}, f32[208,256]{1,0:T(8,128)S(1)}, ...), branch_computations={%region_21.21_spmd, %region_22.22_spmd} | conditional | bytes 2588784 | solution.py:429
  38.5 3.8 %collective-permute-start.33 = (f32[208,256]{1,0:T(8,128)S(1)}, f32[208,256]{1,0:T(8,128)S(1)}, u32[]{:S(2)}, u32[]{:S(2)}) collective-permute-start(f32[208,256]{1,0:T(8,128)S(1)} %get-tuple-element.403), channel_id=1, source_target_pairs={{1,0},{2,1},{3,2},{4,3},{5,4},{6,5},{7,6},{8,7},{9,8},{10,9},{11,1... | collective-permute-start | bytes 638984 | tf_op jit(solution)/shard_map/while/body/eval_jaxpr/cond/branch_1_fun/ppermute | solution.py:352
  42.3 18.2 %all_to_all.9 = f32[16,1,128]{2,1,0:T(1,128)S(1)} all-to-all(f32[16,1,128]{2,1,0:T(1,128)S(1)} %copy.81), channel_id=1, replica_groups=mesh['slab'=16,'flow'=16] {'slab'}, dimensions={0} | all-to-all | bytes 16384 | tf_op jit(solution)/shard_map/while/body/eval_jaxpr/cond/branch_1_fun/all_to_all | solution.py:415
  60.7 0.8 %walls.8 = (f32[5,32,256]{2,1,0:T(8,128)S(1)}, f32[5,32,256]{2,1,0:T(8,128)S(1)}, f32[16,1,128]{2,1,0:T(1,128)S(1)}) custom-call(s32[1]{0:T(128)} %bitcast.4.step_ref.refs_0_, s32[2]{0:T(128)S(1)} %get-tuple-element.649.d_ref, s32[2]{0:T(128)S(1)} %get-tuple-element.650.n_ref, f32[16,1,128]{2,1,0:T(1,128)S(1)} %get-tuple-element.628.g_ref, ...), custom_call_target="tpu_custom_call" | custom-call | tf_op jit(solution)/shard_map/while/body/eval_jaxpr/walls/pallas_call | solution.py:420
  61.5 11.3 %conditional.8 = ((f32[5,32,256]{2,1,0:T(8,128)}, f32[5,32,256]{2,1,0:T(8,128)})) conditional(s32[]{:T(128)} %clamp.23, (s32[]{:T(128)}, f32[5,32,256]{2,1,0:T(8,128)S(1)}, f32[5,32,256]{2,1,0:T(8,128)S(1)}) %tuple.126, (s32[]{:T(128)}, f32[5,32,256]{2,1,0:T(8,128)S(1)}, f32[5,32,256]{2,1,0:T(8,128)S(1)}) %tuple.126, ...), branch_computations={%region_1.5_spmd, %region_6.10_spmd, %region_11.15_spmd, %region_1... | conditional | flops 1 | bytes 1310856 | solution.py:423
  61.6 11.3 %conditional.1 = (f32[5,32,256]{2,1,0:T(8,128)}, f32[5,32,256]{2,1,0:T(8,128)}) conditional(s32[]{:T(128)} %clamp.18, (f32[5,32,256]{2,1,0:T(8,128)S(1)}, f32[5,32,256]{2,1,0:T(8,128)S(1)}) %tuple.82, (f32[5,32,256]{2,1,0:T(8,128)S(1)}, f32[5,32,256]{2,1,0:T(8,128)S(1)}) %tuple.82, (f32[5,32,256]{2,1,0:T(8,128)S(1)}, ...), branch_computations={%region_7.6_spmd, %region_8.7_spmd, %region_9.8_spmd, %region_10.9... | conditional | bytes 1310816 | solution.py:407
  61.6 1.3 %collective-permute-start.8 = (f32[5,32,256]{2,1,0:T(8,128)S(1)}, f32[5,32,256]{2,1,0:T(8,128)}, u32[]{:S(2)}, u32[]{:S(2)}) collective-permute-start(f32[5,32,256]{2,1,0:T(8,128)S(1)} %get-tuple-element.369), channel_id=1, source_target_pairs={{244,0},{245,1},{246,2},{247,3},{248,4},{249,5},{250,6},{251,7},{2... | collective-permute-start | bytes 491528 | tf_op jit(solution)/shard_map/while/body/eval_jaxpr/cond/branch_1_fun/cond/branch_0_fun/ppermute | solution.py:359
  62.9 3.2 %collective-permute-start.9 = (f32[5,32,256]{2,1,0:T(8,128)S(1)}, f32[5,32,256]{2,1,0:T(8,128)}, u32[]{:S(2)}, u32[]{:S(2)}) collective-permute-start(f32[5,32,256]{2,1,0:T(8,128)S(1)} %get-tuple-element.370), channel_id=1, source_target_pairs={{28,0},{29,1},{30,2},{31,3},{16,4},{17,5},{18,6},{19,7},{20,8},{21... | collective-permute-start | bytes 491528 | tf_op jit(solution)/shard_map/while/body/eval_jaxpr/cond/branch_1_fun/cond/branch_0_fun/ppermute | solution.py:359
  66.1 3.6 %collective-permute-done.8 = f32[5,32,256]{2,1,0:T(8,128)} collective-permute-done((f32[5,32,256]{2,1,0:T(8,128)S(1)}, f32[5,32,256]{2,1,0:T(8,128)}, u32[]{:S(2)}, u32[]{:S(2)}) %collective-permute-start.8) | collective-permute-done | bytes 163872 | tf_op jit(solution)/shard_map/while/body/eval_jaxpr/cond/branch_1_fun/cond/branch_0_fun/ppermute | solution.py:359
  69.6 3.2 %collective-permute-done.9 = f32[5,32,256]{2,1,0:T(8,128)} collective-permute-done((f32[5,32,256]{2,1,0:T(8,128)S(1)}, f32[5,32,256]{2,1,0:T(8,128)}, u32[]{:S(2)}, u32[]{:S(2)}) %collective-permute-start.9) | collective-permute-done | bytes 163872 | tf_op jit(solution)/shard_map/while/body/eval_jaxpr/cond/branch_1_fun/cond/branch_0_fun/ppermute | solution.py:359
  72.8 4.9 %following.8 = (f32[19,8,32,256]{3,2,1,0:T(8,128)}, f32[10,32,256]{2,1,0:T(8,128)S(1)}, f32[208,256]{1,0:T(8,128)S(1)}, f32[208,256]{1,0:T(8,128)S(1)}, f32[2,4]{1,0:T(2,128)S(1)}) custom-call(s32[1]{0:T(128)} %bitcast.4.step_ref.refs_0_, f32[19,8,32,256]{3,2,1,0:T(8,128)} %get-tuple-element.624.refs_1_, ...), custom_call_target="tpu_custom_call", output_to_operand_aliasing={{0}: (1, {})} | custom-call | tf_op jit(solution)/shard_map/while/body/eval_jaxpr/following/pallas_call | solution.py:424
  (23 shorter events, 0.9 us)
Async XLA Ops:
  0.6 12.1 %copy-start = (s32[2]{0:T(128)S(1)}, s32[2]{0:T(128)}, u32[]{:S(2)}) copy-start(s32[2]{0:T(128)} %param.28) | copy-start | bytes 28
  0.6 18.1 %copy-start.1 = (s32[2]{0:T(128)S(1)}, s32[2]{0:T(128)}, u32[]{:S(2)}) copy-start(s32[2]{0:T(128)} %param.29) | copy-start | bytes 28
  5.4 13.4 %collective-permute-start.34 = (f32[208,256]{1,0:T(8,128)S(1)}, f32[208,256]{1,0:T(8,128)S(1)}, u32[]{:S(2)}, u32[]{:S(2)}) collective-permute-start(f32[208,256]{1,0:T(8,128)S(1)} %get-tuple-element.440), channel_id=1, source_target_pairs={{15,0},{0,1},{1,2},{2,3},{3,4},{4,5},{5,6},{6,7},{7,8},{8,9},{9,10... | collective-permute-start | bytes 638984 | tf_op jit(solution)/shard_map/ppermute | solution.py:352
  5.5 13.3 %collective-permute-start.35 = (f32[208,256]{1,0:T(8,128)S(1)}, f32[208,256]{1,0:T(8,128)S(1)}, u32[]{:S(2)}, u32[]{:S(2)}) collective-permute-start(f32[208,256]{1,0:T(8,128)S(1)} %get-tuple-element.441), channel_id=1, source_target_pairs={{1,0},{2,1},{3,2},{4,3},{5,4},{6,5},{7,6},{8,7},{9,8},{10,9},{11,1... | collective-permute-start | bytes 638984 | tf_op jit(solution)/shard_map/ppermute | solution.py:352
  9.3 9.4 %all-to-all-start.1 = ((f32[16,1,128]{2,1,0:T(1,128)}), f32[16,1,128]{2,1,0:T(1,128)S(1)}, u32[]{:S(2)}, u32[]{:S(2)}) async-start(f32[16,1,128]{2,1,0:T(1,128)} %get-tuple-element.442), calls=%async_computation.1 | async-start | bytes 16384 | tf_op jit(solution)/shard_map/all_to_all | solution.py:415
  19.8 5.7 %collective-permute-start.6 = (f32[5,32,256]{2,1,0:T(8,128)S(1)}, f32[5,32,256]{2,1,0:T(8,128)}, u32[]{:S(2)}, u32[]{:S(2)}) collective-permute-start(f32[5,32,256]{2,1,0:T(8,128)S(1)} %get-tuple-element.364), channel_id=1, source_target_pairs={{243,0},{244,1},{245,2},{246,3},{247,4},{248,5},{249,6},{250,7},{2... | collective-permute-start | bytes 491528 | tf_op jit(solution)/shard_map/while/body/eval_jaxpr/cond/branch_0_fun/cond/branch_3_fun/ppermute | solution.py:359
  21.9 10.1 %collective-permute-start.7 = (f32[5,32,256]{2,1,0:T(8,128)S(1)}, f32[5,32,256]{2,1,0:T(8,128)}, u32[]{:S(2)}, u32[]{:S(2)}) collective-permute-start(f32[5,32,256]{2,1,0:T(8,128)S(1)} %get-tuple-element.365), channel_id=1, source_target_pairs={{29,0},{30,1},{31,2},{16,3},{17,4},{18,5},{19,6},{20,7},{21,8},{22... | collective-permute-start | bytes 491528 | tf_op jit(solution)/shard_map/while/body/eval_jaxpr/cond/branch_0_fun/cond/branch_3_fun/ppermute | solution.py:359
  38.4 22.2 %collective-permute-start.32 = (f32[208,256]{1,0:T(8,128)S(1)}, f32[208,256]{1,0:T(8,128)S(1)}, u32[]{:S(2)}, u32[]{:S(2)}) collective-permute-start(f32[208,256]{1,0:T(8,128)S(1)} %get-tuple-element.402), channel_id=1, source_target_pairs={{15,0},{0,1},{1,2},{2,3},{3,4},{4,5},{5,6},{6,7},{7,8},{8,9},{9,10... | collective-permute-start | bytes 638984 | tf_op jit(solution)/shard_map/while/body/eval_jaxpr/cond/branch_1_fun/ppermute | solution.py:352
  38.5 22.1 %collective-permute-start.33 = (f32[208,256]{1,0:T(8,128)S(1)}, f32[208,256]{1,0:T(8,128)S(1)}, u32[]{:S(2)}, u32[]{:S(2)}) collective-permute-start(f32[208,256]{1,0:T(8,128)S(1)} %get-tuple-element.403), channel_id=1, source_target_pairs={{1,0},{2,1},{3,2},{4,3},{5,4},{6,5},{7,6},{8,7},{9,8},{10,9},{11,1... | collective-permute-start | bytes 638984 | tf_op jit(solution)/shard_map/while/body/eval_jaxpr/cond/branch_1_fun/ppermute | solution.py:352
  61.6 8.1 %collective-permute-start.8 = (f32[5,32,256]{2,1,0:T(8,128)S(1)}, f32[5,32,256]{2,1,0:T(8,128)}, u32[]{:S(2)}, u32[]{:S(2)}) collective-permute-start(f32[5,32,256]{2,1,0:T(8,128)S(1)} %get-tuple-element.369), channel_id=1, source_target_pairs={{244,0},{245,1},{246,2},{247,3},{248,4},{249,5},{250,6},{251,7},{2... | collective-permute-start | bytes 491528 | tf_op jit(solution)/shard_map/while/body/eval_jaxpr/cond/branch_1_fun/cond/branch_0_fun/ppermute | solution.py:359
  62.9 9.9 %collective-permute-start.9 = (f32[5,32,256]{2,1,0:T(8,128)S(1)}, f32[5,32,256]{2,1,0:T(8,128)}, u32[]{:S(2)}, u32[]{:S(2)}) collective-permute-start(f32[5,32,256]{2,1,0:T(8,128)S(1)} %get-tuple-element.370), channel_id=1, source_target_pairs={{28,0},{29,1},{30,2},{31,3},{16,4},{17,5},{18,6},{19,7},{20,8},{21... | collective-permute-start | bytes 491528 | tf_op jit(solution)/shard_map/while/body/eval_jaxpr/cond/branch_1_fun/cond/branch_0_fun/ppermute | solution.py:359
where the time goes:
time: 79.6 us; the launch traced here: 78.4 us
  waiting for transfers between devices  20.8 us (26%)
  blocking collectives  18.2 us (23%)
  starting transfers between devices  17.8 us (22%)
  Pallas kernels  17.7 us (22%)
  between operations  2.05 us (3%)
  local copies, waits for them, and re-layouts  1.32 us (2%)
    all_to_all x1, blocking collectives, neighbours(): return (from_left, from_right, lax.all_to_all(sums, axis, 0, 0))  18.2 us
    ppermute x4, waiting for transfers between devices, displaced(): return lax.ppermute(value, both, route)  16.8 us
    pallas_call x2, Pallas kernels, step(): following(at, pltpu.with_memory_space_constraint(p, pltpu.HBM), *kept(fro...  11.3 us
    ppermute x4, starting transfers between devices, beside(): return lax.ppermute(value, 'flow', route)  7.85 us
    ppermute x4, starting transfers between devices, displaced(): return lax.ppermute(value, both, route)  6.53 us
    pallas_call x1, Pallas kernels, local(): first(pltpu.with_memory_space_constraint(populations, pltpu.HBM))  4.71 us
    all_to_all x1, waiting for transfers between devices, neighbours(): return (from_left, from_right, lax.all_to_all(sums, axis, 0, 0))  4 us
    all_to_all x1, starting transfers between devices, neighbours(): return (from_left, from_right, lax.all_to_all(sums, axis, 0, 0))  3.41 us
  transfers between devices with their start and end apart: 9, of which 5 were waited for; matrix products, arithmetic and copies ran while one was open for 1% of the time, Pallas kernels for 0%

commit v1 on v0

--- a/solution.py
+++ b/solution.py
@@ -42,6 +42,7 @@
 HALO = 10 * REACH
 EXTRA = HALO + 40
 ROWS = EXTRA + 8
+STRIDE = 4
 
 
 def moments(f):
@@ -160,7 +161,23 @@
         message[EXTRA:ROWS, :] = jnp.zeros((ROWS - EXTRA, message.shape[1]), jnp.float32)
 
 
-def first_kernel(f_hbm, p_hbm, e_ref, mr_ref, ml_ref, t_ref, f_ref, p_ref, acc_ref, in_sems, out_sems):
+def first_kernel(
+    f_hbm,
+    p_hbm,
+    e_ref,
+    mr_ref,
+    ml_ref,
+    t_ref,
+    t0_ref,
+    t1_ref,
+    t2_ref,
+    t3_ref,
+    f_ref,
+    p_ref,
+    acc_ref,
+    in_sems,
+    out_sems,
+):
     slab_rows = f_ref.shape[1]
 
     def arriving(y):
@@ -173,6 +190,8 @@
         arriving(y).start()
     acc_ref[...] = jnp.zeros_like(acc_ref)
     clear_rest(mr_ref, ml_ref)
+    for table in (t0_ref, t1_ref, t2_ref, t3_ref):
+        table[...] = jnp.zeros_like(table)
 
     def load(y, lo):
         return [f_ref[n, y, lo : lo + 8, :] for n in range(19)]
@@ -203,9 +222,9 @@
         out = []
         for n, (c_x, c_y, c_z) in enumerate(VELOCITY):
             if c_y == 1 and isinstance(y, int) and y == 0:
-                v = wu[UPWARD.index(n), lo : lo + 8, :]
+                v = wu[UPWARD.index(n) * cells + lo : UPWARD.index(n) * cells + lo + 8, :]
             elif c_y == -1 and isinstance(y, int) and y == slab_rows - 1:
-                v = wd[DOWNWARD.index(n), lo : lo + 8, :]
+                v = wd[DOWNWARD.index(n) * cells + lo : DOWNWARD.index(n) * cells + lo + 8, :]
             elif c_x == 1 and lo == 0:
                 halo = rl[pl.ds(HALO + 8 * RIGHTWARD.index(n) + y - c_y, 1), :]
                 v = jnp.where(row == 0, halo, pltpu.roll(p_ref[n, y - c_y, 0:8, :], 1, axis=0))
@@ -225,16 +244,18 @@
 def next_kernel(
     all_cells,
     step_ref,
+    slab_ref,
     p_hbm,
     rl,
     rr,
     wu,
     wd,
-    g_ref,
+    up_ref,
     o_hbm,
     e_ref,
     mr_ref,
     ml_ref,
+    t_ref,
     s_ref,
     p_ref,
     q_ref,
@@ -252,7 +273,11 @@
     for y in range(slab_rows):
         arriving(y).start()
     clear_rest(mr_ref, ml_ref)
-    total = g_ref[0] * (1.0 / all_cells)
+    known, below, above = (ref[5 * cells :, :] for ref in (up_ref, wu, wd))
+    t_ref[...] = known + below + above
+    ahead = (slab_rows_of(known.shape) - slab_ref[0]) & (STRIDE - 1)
+    total = jnp.sum(jnp.where(ahead == 2, above, known), axis=0, keepdims=True)
+    total = (total[:, :128] + total[:, 128:]) * (1.0 / all_cells)
     lane = lax.broadcasted_iota(jnp.int32, total.shape, 1)
     rho, m_x, m_y, m_z, first, second = (
         jnp.sum(jnp.where(lane == q, total, 0.0)) for q in range(6)
@@ -295,13 +320,40 @@
         leaving(y).wait()
 
 
-def wall_kernel(step_ref, d_ref, n_ref, g_ref, e_ref, rl, rr, up_ref, down_ref, t_ref, s_ref):
+def slab_rows_of(shape):
+    half = jnp.where(lax.broadcasted_iota(jnp.int32, shape, 1) >= shape[1] // 2, 1, 0)
+    return lax.broadcasted_iota(jnp.int32, shape, 0) + shape[0] * half
+
+
+def wall_kernel(
+    step_ref,
+    slab_ref,
+    d_ref,
+    n_ref,
+    g_ref,
+    own_ref,
+    t1_ref,
+    t2_ref,
+    t3_ref,
+    e_ref,
+    rl,
+    rr,
+    up_ref,
+    down_ref,
+    s_ref,
+):
     cells = e_ref.shape[1]
     own = REACH + 8
     section = step_ref[0]
     r = lax.rem(d_ref[section] + REACH, cells) - REACH
     a = n_ref[section].astype(jnp.float32) * (1.0 / DEN)
-    t_ref[...] = jnp.broadcast_to(jnp.sum(g_ref[...], axis=0, keepdims=True), t_ref.shape)
+    local = jnp.sum(g_ref[...], axis=0)
+    local = jnp.broadcast_to(jnp.concatenate([local, local], axis=1), own_ref.shape)
+    local = jnp.where(slab_rows_of(own_ref.shape) == slab_ref[0], local, 0.0)
+    known = own_ref[...] + t1_ref[...] + t2_ref[...] + t3_ref[...]
+    known = jnp.where(section == 0, local, known)
+    up_ref[5 * cells :, :] = known
+    down_ref[5 * cells :, :] = known
     for j, n in enumerate(EDGES):
         side, c_x = j // 5, VELOCITY[n][0]
         s_ref[8:own, :] = rl[j * REACH : (j + 1) * REACH, :]
@@ -322,7 +374,8 @@
         line = s_ref[...]
         count = line.shape[0]
         line = low * line + high * pltpu.roll(line, count - 1, axis=0)
-        out[j % 5] = pltpu.roll(line, count - start, axis=0)[:cells]
+        at = (j % 5) * cells
+        out[at : at + cells, :] = pltpu.roll(line, count - start, axis=0)[:cells]
 
 
 VMEM = pl.BlockSpec(memory_space=pltpu.VMEM)
@@ -343,7 +396,8 @@
     _, slab_rows, cells, depth = shape = populations.shape
     slabs, flows = lax.axis_size("slab"), lax.axis_size("flow")
     all_cells = slab_rows * cells * depth * slabs * flows
-    side = (5, cells, depth)
+    side = (5 * cells + 8, depth)
+    table = (8, depth)
     both = ("slab", "flow")
     everyone = [(s, f) for s in range(slabs) for f in range(flows)]
 
@@ -369,29 +423,29 @@
 
     first = pl.pallas_call(
         first_kernel,
-        out_shape=(state,) + edge_outs + (near(flows, 1, 128),),
+        out_shape=(state,) + edge_outs + (near(flows, 1, 128),) + (near(*table),) * 4,
         in_specs=[HBM],
-        out_specs=(HBM,) + (VMEM,) * 4,
+        out_specs=(HBM,) + (VMEM,) * 8,
         scratch_shapes=buffers + [pltpu.VMEM((6, 8, depth), jnp.float32)] + row_sems,
         compiler_params=PARAMS,
         name="first",
     )
     walls = pl.pallas_call(
         wall_kernel,
-        out_shape=(near(*side), near(*side), near(slabs, 1, 128)),
-        in_specs=[SMEM] * 3 + [VMEM] * 4,
-        out_specs=(VMEM,) * 3,
+        out_shape=(near(*side), near(*side)),
+        in_specs=[SMEM] * 4 + [VMEM] * 8,
+        out_specs=(VMEM,) * 2,
         scratch_shapes=[pltpu.VMEM((cells + 2 * REACH + 16, depth), jnp.float32)],
         compiler_params=PARAMS,
         name="walls",
     )
     following = pl.pallas_call(
         lambda *refs: next_kernel(all_cells, *refs),
-        out_shape=(state,) + edge_outs + (near(STEPS, 4),),
-        in_specs=[SMEM, HBM] + [VMEM] * 5,
-        out_specs=(HBM,) + (VMEM,) * 4,
+        out_shape=(state,) + edge_outs + (near(*table), near(STEPS, 4)),
+        in_specs=[SMEM, SMEM, HBM] + [VMEM] * 5,
+        out_specs=(HBM,) + (VMEM,) * 5,
         scratch_shapes=buffers + row_sems,
-        input_output_aliases={1: 0},
+        input_output_aliases={2: 0},
         compiler_params=PARAMS,
         name="following",
     )
@@ -410,36 +464,50 @@
     branches = [twig(start, count) for start in range(0, flows, count)]
     blocks = [((offsets[k] + REACH) // cells) % flows for k in range(STEPS)]
 
-    def neighbours(axis, mr, ml, sums):
-        from_left, from_right = beside(mr, 1), beside(ml, -1)
-        return from_left, from_right, lax.all_to_all(sums, axis, 0, 0)
+    slab = lax.axis_index("slab").reshape(1)
+
+    def neighbours(mr, ml):
+        return beside(mr, 1), beside(ml, -1)
+
+    def apart(value, distance):
+        return lax.ppermute(value, "slab", [(i, (i + distance) % slabs) for i in range(slabs)])
 
     def step(section, carry):
-        p, edges, from_left, from_right, gathered, _, now, *later = carry
+        p, edges, from_left, from_right, tables, _, now, *later = carry
         at = section.reshape(1)
-        up, down, sums = walls(
-            at, offsets, fraction, *kept(gathered, edges, from_left, from_right)
+        up, down = walls(
+            at,
+            slab,
+            offsets,
+            fraction,
+            *kept(gathered, *tables, edges, from_left, from_right),
         )
         wu, wd = lax.switch(now // count, branches, now % count, up, down)
-        p, edges, mr, ml, totals = following(
+        p, edges, mr, ml, known, totals = following(
             at,
+            slab,
             pltpu.with_memory_space_constraint(p, pltpu.HBM),
-            *kept(from_left, from_right, wu, wd, sums),
+            *kept(from_left, from_right, wu, wd, up),
         )
-        from_left, from_right, gathered = lax.cond(
+        from_left, from_right, tables = lax.cond(
             section < STEPS - 1,
-            lambda mr, ml, sums: neighbours("slab", mr, ml, sums),
-            lambda mr, ml, sums: (mr, ml, sums),
+            lambda mr, ml, known, _: (
+                *neighbours(mr, ml),
+                (known, *(apart(known, k * STRIDE) for k in range(1, slabs // STRIDE))),
+            ),
+            lambda mr, ml, known, tables: (mr, ml, tables),
             mr,
             ml,
-            sums,
+            known,
+            tables,
         )
-        return p, edges, from_left, from_right, gathered, totals, *later, now
-
-    p, edges, mr, ml, sums = first(pltpu.with_memory_space_constraint(populations, pltpu.HBM))
-    from_left, from_right, gathered = neighbours("flow", mr, ml, sums)
+        return p, edges, from_left, from_right, tables, totals, *later, now
+
+    p, edges, mr, ml, sums, *tables = first(pltpu.with_memory_space_constraint(populations, pltpu.HBM))
+    from_left, from_right = neighbours(mr, ml)
+    gathered = lax.all_to_all(sums, "flow", 0, 0)
     totals = jnp.zeros((STEPS, 4), jnp.float32)
-    carry = (p, edges, from_left, from_right, gathered, totals, *blocks)
+    carry = (p, edges, from_left, from_right, tuple(tables), totals, *blocks)
     carry = lax.fori_loop(0, STEPS, step, carry)
     return carry[0], carry[5]
 

time: 79.6 us -> 83.8 us (1.053)
  the two profiles are of different devices: /device:TPU:4 before, /device:TPU:1 now
where the time goes in v1:
time: 83.8 us; the launch traced here: 83.3 us
  starting transfers between devices  41.3 us (49%)
  waiting for transfers between devices  20 us (24%)
  Pallas kernels  18.1 us (22%)
  between operations  2.06 us (2%)
  local copies, waits for them, and re-layouts  1.25 us (1%)
    ppermute x4, starting transfers between devices, displaced(): return lax.ppermute(value, both, route)  19.4 us
    ppermute x4, waiting for transfers between devices, displaced(): return lax.ppermute(value, both, route)  15.7 us
    pallas_call x2, Pallas kernels, step(): following(at, slab, pltpu.with_memory_space_constraint(p, pltpu.HBM), *ke...  11.3 us
    ppermute x3, starting transfers between devices, apart(): lax.ppermute(value, 'slab', [(i, (i + distance) % slabs) for i in range(s...  9.69 us
    all_to_all x1, starting transfers between devices, local(): gathered = lax.all_to_all(sums, 'flow', 0, 0)  7.03 us
    ppermute x4, starting transfers between devices, beside(): return lax.ppermute(value, 'flow', route)  5.12 us
    pallas_call x1, Pallas kernels, local(): first(pltpu.with_memory_space_constraint(populations, pltpu.HBM))  4.73 us
    all_to_all x1, waiting for transfers between devices, local(): gathered = lax.all_to_all(sums, 'flow', 0, 0)  3.55 us
  transfers between devices with their start and end apart: 12, of which 5 were waited for; matrix products, arithmetic and copies ran while one was open for 1% of the time, Pallas kernels for 0%

profile of v1, /device:TPU:1, one launch (start us, length us, event | category | flops | bytes accessed | tf_op | source)
XLA Modules:
  0.0 83.3 jit_solution(4760220568884027978)
XLA Ops:
  0.6 4.7 %first.1 = (f32[19,8,32,256]{3,2,1,0:T(8,128)}, f32[10,32,256]{2,1,0:T(8,128)S(1)}, f32[208,256]{1,0:T(8,128)S(1)}, f32[208,256]{1,0:T(8,128)S(1)}, f32[16,1,128...) custom-call(f32[19,8,32,256]{3,2,1,0:T(8,128)} %f_hbm.1), custom_call_target="tpu_custom_call" | custom-call | tf_op jit(solution)/shard_map/first/pallas_call | solution.py:506
  5.4 2.7 %collective-permute-start.37 = (f32[208,256]{1,0:T(8,128)S(1)}, f32[208,256]{1,0:T(8,128)S(1)}, u32[]{:S(2)}, u32[]{:S(2)}) collective-permute-start(f32[208,256]{1,0:T(8,128)S(1)} %get-tuple-element.565), channel_id=1, source_target_pairs={{15,0},{0,1},{1,2},{2,3},{3,4},{4,5},{5,6},{6,7},{7,8},{8,9},{9,10... | collective-permute-start | bytes 638984 | tf_op jit(solution)/shard_map/ppermute | solution.py:406
  8.8 7.0 %all-to-all-start = ((f32[16,1,128]{2,1,0:T(1,128)}), f32[16,1,128]{2,1,0:T(1,128)S(1)}, u32[]{:S(2)}, u32[]{:S(2)}) async-start(f32[16,1,128]{2,1,0:T(1,128)} %get-tuple-element.571), calls=%async_computation | async-start | bytes 16384 | tf_op jit(solution)/shard_map/all_to_all | solution.py:508
  17.8 3.6 %all-to-all-done = f32[16,1,128]{2,1,0:T(1,128)S(1)} async-done(((f32[16,1,128]{2,1,0:T(1,128)}), f32[16,1,128]{2,1,0:T(1,128)S(1)}, u32[]{:S(2)}, u32[]{:S(2)}) %all-to-all-start) | async-done | bytes 8224 | tf_op jit(solution)/shard_map/all_to_all | solution.py:508
  21.4 61.3 %while.35 = (s32[]{:T(128)}, f32[19,8,32,256]{3,2,1,0:T(8,128)}, f32[10,32,256]{2,1,0:T(8,128)S(1)}, f32[208,256]{1,0:T(8,128)S(1)}, f32[208,256]{1,0:T(8,128)S(...) while((s32[]{:T(128)}, f32[19,8,32,256]{3,2,1,0:T(8,128)}, ...), condition=%wide.region_23.24_spmd, body=%wide.region_0.23_spmd.sunk | while | flops 25 | bytes 4899742 | solution.py:511
  21.6 1.0 %walls.8 = (f32[168,256]{1,0:T(8,128)S(1)}, f32[168,256]{1,0:T(8,128)S(1)}) custom-call(s32[1]{0:T(128)} %bitcast.5.step_ref.refs_0_, s32[1]{0:T(128)} %get-tuple-element.843.slab_ref.refs_1_, s32[2]{0:T(128)S(1)} %get-tuple-element.844.d_ref, s32[2]{0:T(128)S(1)} %get-tuple-element.845.n_ref, f32[16,1,128]{2,1,0:T(1,128)S(1)} %get-tuple-element.846.g_ref, ...), custom_call_target="tpu_custom_call" | custom-call | tf_op jit(solution)/shard_map/while/body/eval_jaxpr/walls/pallas_call | solution.py:478
  22.7 18.5 %conditional.8 = ((f32[168,256]{1,0:T(8,128)}, f32[168,256]{1,0:T(8,128)})) conditional(s32[]{:T(128)} %clamp.23, (s32[]{:T(128)}, f32[168,256]{1,0:T(8,128)S(1)}, f32[168,256]{1,0:T(8,128)S(1)}) %tuple.127, (s32[]{:T(128)}, f32[168,256]{1,0:T(8,128)S(1)}, f32[168,256]{1,0:T(8,128)S(1)}) %tuple.127, (s32[]{:T(128)}, ...), branch_computations={%region_1.5_spmd, %region_6.10_spmd, %region_11.15_spmd, %region_1... | conditional | flops 1 | bytes 1376392 | solution.py:485
  22.7 18.5 %conditional.3 = (f32[168,256]{1,0:T(8,128)}, f32[168,256]{1,0:T(8,128)}) conditional(s32[]{:T(128)} %clamp.20, (f32[168,256]{1,0:T(8,128)S(1)}, f32[168,256]{1,0:T(8,128)S(1)}) %tuple.98, (f32[168,256]{1,0:T(8,128)S(1)}, f32[168,256]{1,0:T(8,128)S(1)}) %tuple.98, (f32[168,256]{1,0:T(8,128)S(1)}, ...), branch_computations={%region_17.16_spmd, %region_18.17_spmd, %region_19.18_spmd, %regio... | conditional | bytes 1376352 | solution.py:461
  22.9 11.1 %collective-permute-start.29 = (f32[168,256]{1,0:T(8,128)S(1)}, f32[168,256]{1,0:T(8,128)}, u32[]{:S(2)}, u32[]{:S(2)}) collective-permute-start(f32[168,256]{1,0:T(8,128)S(1)} %get-tuple-element.509), channel_id=1, source_target_pairs={{18,0},{19,1},{20,2},{21,3},{22,4},{23,5},{24,6},{25,7},{26,8},{27... | collective-permute-start | bytes 516104 | tf_op jit(solution)/shard_map/while/body/eval_jaxpr/cond/branch_3_fun/cond/branch_2_fun/ppermute | solution.py:413
  34.0 7.2 %collective-permute-done.29 = f32[168,256]{1,0:T(8,128)} collective-permute-done((f32[168,256]{1,0:T(8,128)S(1)}, f32[168,256]{1,0:T(8,128)}, u32[]{:S(2)}, u32[]{:S(2)}) %collective-permute-start.29) | collective-permute-done | bytes 172064 | tf_op jit(solution)/shard_map/while/body/eval_jaxpr/cond/branch_3_fun/cond/branch_2_fun/ppermute | solution.py:413
  41.2 6.4 %following.8 = (f32[19,8,32,256]{3,2,1,0:T(8,128)}, f32[10,32,256]{2,1,0:T(8,128)S(1)}, f32[208,256]{1,0:T(8,128)S(1)}, f32[208,256]{1,0:T(8,128)S(1)}, f32[8,256]{1,0:T(8,128)S(1)}, /*index=5*/f32[2,4]{1,0:T(2,128)S(1)}) custom-call(s32[1]{0:T(128)} %bitcast.5.step_ref.refs_0_, ...), custom_call_target="tpu_custom_call", output_to_operand_aliasing={{0}: (2, {})} | custom-call | tf_op jit(solution)/shard_map/while/body/eval_jaxpr/following/pallas_call | solution.py:486
  47.6 12.2 %conditional.9 = ((f32[208,256]{1,0:T(8,128)S(1)}, f32[208,256]{1,0:T(8,128)S(1)}, f32[8,256]{1,0:T(8,128)S(1)}, f32[8,256]{1,0:T(8,128)}, f32[8,256]{1,0:T(8,128)}, /*index=5*/f32[8,256]{1,0:T(8,128)})) conditional(s32[]{:T(128)} %convert_element_type.11, (f32[208,256]{1,0:T(8,128)S(1)}, f32[208,256]{1,0:T(8,128)S(1)}, f32[8,256]{1,0:T(8,128)S(1)}, ...), branch_computations={%region_21.21_spmd, %region_22.22_spmd} | conditional | bytes 2670848 | solution.py:492
  47.6 1.7 %collective-permute-start.32 = (f32[208,256]{1,0:T(8,128)S(1)}, f32[208,256]{1,0:T(8,128)S(1)}, u32[]{:S(2)}, u32[]{:S(2)}) collective-permute-start(f32[208,256]{1,0:T(8,128)S(1)} %get-tuple-element.515), channel_id=1, source_target_pairs={{15,0},{0,1},{1,2},{2,3},{3,4},{4,5},{5,6},{6,7},{7,8},{8,9},{9,10... | collective-permute-start | bytes 638984 | tf_op jit(solution)/shard_map/while/body/eval_jaxpr/cond/branch_1_fun/ppermute | solution.py:406
  49.3 2.6 %collective-permute-start.34 = (f32[8,256]{1,0:T(8,128)S(1)}, f32[8,256]{1,0:T(8,128)}, u32[]{:S(2)}, u32[]{:S(2)}) collective-permute-start(f32[8,256]{1,0:T(8,128)S(1)} %get-tuple-element.783), channel_id=1, source_target_pairs={{0,64},{16,80},{32,96},{48,112},{64,128},{80,144},{96,160},{112,17... | collective-permute-start | bytes 24584 | tf_op jit(solution)/shard_map/while/body/eval_jaxpr/cond/branch_1_fun/ppermute | solution.py:473
  51.9 4.4 %collective-permute-start.35 = (f32[8,256]{1,0:T(8,128)S(1)}, f32[8,256]{1,0:T(8,128)}, u32[]{:S(2)}, u32[]{:S(2)}) collective-permute-start(f32[8,256]{1,0:T(8,128)S(1)} %get-tuple-element.783), channel_id=1, source_target_pairs={{0,128},{16,144},{32,160},{48,176},{64,192},{80,208},{96,224},{112... | collective-permute-start | bytes 24584 | tf_op jit(solution)/shard_map/while/body/eval_jaxpr/cond/branch_1_fun/ppermute | solution.py:473
  56.3 2.8 %collective-permute-start.36 = (f32[8,256]{1,0:T(8,128)S(1)}, f32[8,256]{1,0:T(8,128)}, u32[]{:S(2)}, u32[]{:S(2)}) collective-permute-start(f32[8,256]{1,0:T(8,128)S(1)} %get-tuple-element.783), channel_id=1, source_target_pairs={{0,192},{16,208},{32,224},{48,240},{64,0},{80,16},{96,32},{112,48}... | collective-permute-start | bytes 24584 | tf_op jit(solution)/shard_map/while/body/eval_jaxpr/cond/branch_1_fun/ppermute | solution.py:473
  59.9 1.0 %walls.8 = (f32[168,256]{1,0:T(8,128)S(1)}, f32[168,256]{1,0:T(8,128)S(1)}) custom-call(s32[1]{0:T(128)} %bitcast.5.step_ref.refs_0_, s32[1]{0:T(128)} %get-tuple-element.843.slab_ref.refs_1_, s32[2]{0:T(128)S(1)} %get-tuple-element.844.d_ref, s32[2]{0:T(128)S(1)} %get-tuple-element.845.n_ref, f32[16,1,128]{2,1,0:T(1,128)S(1)} %get-tuple-element.846.g_ref, ...), custom_call_target="tpu_custom_call" | custom-call | tf_op jit(solution)/shard_map/while/body/eval_jaxpr/walls/pallas_call | solution.py:478
  61.0 16.8 %conditional.8 = ((f32[168,256]{1,0:T(8,128)}, f32[168,256]{1,0:T(8,128)})) conditional(s32[]{:T(128)} %clamp.23, (s32[]{:T(128)}, f32[168,256]{1,0:T(8,128)S(1)}, f32[168,256]{1,0:T(8,128)S(1)}) %tuple.127, (s32[]{:T(128)}, f32[168,256]{1,0:T(8,128)S(1)}, f32[168,256]{1,0:T(8,128)S(1)}) %tuple.127, (s32[]{:T(128)}, ...), branch_computations={%region_1.5_spmd, %region_6.10_spmd, %region_11.15_spmd, %region_1... | conditional | flops 1 | bytes 1376392 | solution.py:485
  61.0 16.7 %conditional.1 = (f32[168,256]{1,0:T(8,128)}, f32[168,256]{1,0:T(8,128)}) conditional(s32[]{:T(128)} %clamp.18, (f32[168,256]{1,0:T(8,128)S(1)}, f32[168,256]{1,0:T(8,128)S(1)}) %tuple.82, (f32[168,256]{1,0:T(8,128)S(1)}, f32[168,256]{1,0:T(8,128)S(1)}) %tuple.82, (f32[168,256]{1,0:T(8,128)S(1)}, ...), branch_computations={%region_7.6_spmd, %region_8.7_spmd, %region_9.8_spmd, %region_10.9... | conditional | bytes 1376352 | solution.py:461
  61.0 6.6 %collective-permute-start.10 = (f32[168,256]{1,0:T(8,128)S(1)}, f32[168,256]{1,0:T(8,128)}, u32[]{:S(2)}, u32[]{:S(2)}) collective-permute-start(f32[168,256]{1,0:T(8,128)S(1)} %get-tuple-element.484), channel_id=1, source_target_pairs={{245,0},{246,1},{247,2},{248,3},{249,4},{250,5},{251,6},{252,7},{2... | collective-permute-start | bytes 516104 | tf_op jit(solution)/shard_map/while/body/eval_jaxpr/cond/branch_1_fun/cond/branch_1_fun/ppermute | solution.py:413
  67.6 1.6 %collective-permute-start.11 = (f32[168,256]{1,0:T(8,128)S(1)}, f32[168,256]{1,0:T(8,128)}, u32[]{:S(2)}, u32[]{:S(2)}) collective-permute-start(f32[168,256]{1,0:T(8,128)S(1)} %get-tuple-element.485), channel_id=1, source_target_pairs={{27,0},{28,1},{29,2},{30,3},{31,4},{16,5},{17,6},{18,7},{19,8},{20... | collective-permute-start | bytes 516104 | tf_op jit(solution)/shard_map/while/body/eval_jaxpr/cond/branch_1_fun/cond/branch_1_fun/ppermute | solution.py:413
  69.1 5.3 %collective-permute-done.10 = f32[168,256]{1,0:T(8,128)} collective-permute-done((f32[168,256]{1,0:T(8,128)S(1)}, f32[168,256]{1,0:T(8,128)}, u32[]{:S(2)}, u32[]{:S(2)}) %collective-permute-start.10) | collective-permute-done | bytes 172064 | tf_op jit(solution)/shard_map/while/body/eval_jaxpr/cond/branch_1_fun/cond/branch_1_fun/ppermute | solution.py:413
  74.4 3.3 %collective-permute-done.11 = f32[168,256]{1,0:T(8,128)} collective-permute-done((f32[168,256]{1,0:T(8,128)S(1)}, f32[168,256]{1,0:T(8,128)}, u32[]{:S(2)}, u32[]{:S(2)}) %collective-permute-start.11) | collective-permute-done | bytes 172064 | tf_op jit(solution)/shard_map/while/body/eval_jaxpr/cond/branch_1_fun/cond/branch_1_fun/ppermute | solution.py:413
  77.7 4.9 %following.8 = (f32[19,8,32,256]{3,2,1,0:T(8,128)}, f32[10,32,256]{2,1,0:T(8,128)S(1)}, f32[208,256]{1,0:T(8,128)S(1)}, f32[208,256]{1,0:T(8,128)S(1)}, f32[8,256]{1,0:T(8,128)S(1)}, /*index=5*/f32[2,4]{1,0:T(2,128)S(1)}) custom-call(s32[1]{0:T(128)} %bitcast.5.step_ref.refs_0_, ...), custom_call_target="tpu_custom_call", output_to_operand_aliasing={{0}: (2, {})} | custom-call | tf_op jit(solution)/shard_map/while/body/eval_jaxpr/following/pallas_call | solution.py:486
  (26 shorter events, 2.9 us)
Async XLA Ops:
  0.6 15.2 %copy-start = (s32[2]{0:T(128)S(1)}, s32[2]{0:T(128)}, u32[]{:S(2)}) copy-start(s32[2]{0:T(128)} %param.28) | copy-start | bytes 28
  0.6 20.7 %copy-start.1 = (s32[2]{0:T(128)S(1)}, s32[2]{0:T(128)}, u32[]{:S(2)}) copy-start(s32[2]{0:T(128)} %param.29) | copy-start | bytes 28
  5.4 16.0 %collective-permute-start.37 = (f32[208,256]{1,0:T(8,128)S(1)}, f32[208,256]{1,0:T(8,128)S(1)}, u32[]{:S(2)}, u32[]{:S(2)}) collective-permute-start(f32[208,256]{1,0:T(8,128)S(1)} %get-tuple-element.565), channel_id=1, source_target_pairs={{15,0},{0,1},{1,2},{2,3},{3,4},{4,5},{5,6},{6,7},{7,8},{8,9},{9,10... | collective-permute-start | bytes 638984 | tf_op jit(solution)/shard_map/ppermute | solution.py:406
  8.1 13.3 %collective-permute-start.38 = (f32[208,256]{1,0:T(8,128)S(1)}, f32[208,256]{1,0:T(8,128)S(1)}, u32[]{:S(2)}, u32[]{:S(2)}) collective-permute-start(f32[208,256]{1,0:T(8,128)S(1)} %get-tuple-element.566), channel_id=1, source_target_pairs={{1,0},{2,1},{3,2},{4,3},{5,4},{6,5},{7,6},{8,7},{9,8},{10,9},{11,1... | collective-permute-start | bytes 638984 | tf_op jit(solution)/shard_map/ppermute | solution.py:406
  8.8 12.6 %all-to-all-start = ((f32[16,1,128]{2,1,0:T(1,128)}), f32[16,1,128]{2,1,0:T(1,128)S(1)}, u32[]{:S(2)}, u32[]{:S(2)}) async-start(f32[16,1,128]{2,1,0:T(1,128)} %get-tuple-element.571), calls=%async_computation | async-start | bytes 16384 | tf_op jit(solution)/shard_map/all_to_all | solution.py:508
  22.7 11.3 %collective-permute-start.28 = (f32[168,256]{1,0:T(8,128)S(1)}, f32[168,256]{1,0:T(8,128)}, u32[]{:S(2)}, u32[]{:S(2)}) collective-permute-start(f32[168,256]{1,0:T(8,128)S(1)} %get-tuple-element.508), channel_id=1, source_target_pairs={{254,0},{255,1},{240,2},{241,3},{242,4},{243,5},{244,6},{245,7},{2... | collective-permute-start | bytes 516104 | tf_op jit(solution)/shard_map/while/body/eval_jaxpr/cond/branch_3_fun/cond/branch_2_fun/ppermute | solution.py:413
  22.9 18.2 %collective-permute-start.29 = (f32[168,256]{1,0:T(8,128)S(1)}, f32[168,256]{1,0:T(8,128)}, u32[]{:S(2)}, u32[]{:S(2)}) collective-permute-start(f32[168,256]{1,0:T(8,128)S(1)} %get-tuple-element.509), channel_id=1, source_target_pairs={{18,0},{19,1},{20,2},{21,3},{22,4},{23,5},{24,6},{25,7},{26,8},{27... | collective-permute-start | bytes 516104 | tf_op jit(solution)/shard_map/while/body/eval_jaxpr/cond/branch_3_fun/cond/branch_2_fun/ppermute | solution.py:413
  47.6 11.4 %collective-permute-start.32 = (f32[208,256]{1,0:T(8,128)S(1)}, f32[208,256]{1,0:T(8,128)S(1)}, u32[]{:S(2)}, u32[]{:S(2)}) collective-permute-start(f32[208,256]{1,0:T(8,128)S(1)} %get-tuple-element.515), channel_id=1, source_target_pairs={{15,0},{0,1},{1,2},{2,3},{3,4},{4,5},{5,6},{6,7},{7,8},{8,9},{9,10... | collective-permute-start | bytes 638984 | tf_op jit(solution)/shard_map/while/body/eval_jaxpr/cond/branch_1_fun/ppermute | solution.py:406
  49.3 9.7 %collective-permute-start.33 = (f32[208,256]{1,0:T(8,128)S(1)}, f32[208,256]{1,0:T(8,128)S(1)}, u32[]{:S(2)}, u32[]{:S(2)}) collective-permute-start(f32[208,256]{1,0:T(8,128)S(1)} %get-tuple-element.516), channel_id=1, source_target_pairs={{1,0},{2,1},{3,2},{4,3},{5,4},{6,5},{7,6},{8,7},{9,8},{10,9},{11,1... | collective-permute-start | bytes 638984 | tf_op jit(solution)/shard_map/while/body/eval_jaxpr/cond/branch_1_fun/ppermute | solution.py:406
  49.3 9.8 %collective-permute-start.34 = (f32[8,256]{1,0:T(8,128)S(1)}, f32[8,256]{1,0:T(8,128)}, u32[]{:S(2)}, u32[]{:S(2)}) collective-permute-start(f32[8,256]{1,0:T(8,128)S(1)} %get-tuple-element.783), channel_id=1, source_target_pairs={{0,64},{16,80},{32,96},{48,112},{64,128},{80,144},{96,160},{112,17... | collective-permute-start | bytes 24584 | tf_op jit(solution)/shard_map/while/body/eval_jaxpr/cond/branch_1_fun/ppermute | solution.py:473
  51.9 7.2 %collective-permute-start.35 = (f32[8,256]{1,0:T(8,128)S(1)}, f32[8,256]{1,0:T(8,128)}, u32[]{:S(2)}, u32[]{:S(2)}) collective-permute-start(f32[8,256]{1,0:T(8,128)S(1)} %get-tuple-element.783), channel_id=1, source_target_pairs={{0,128},{16,144},{32,160},{48,176},{64,192},{80,208},{96,224},{112... | collective-permute-start | bytes 24584 | tf_op jit(solution)/shard_map/while/body/eval_jaxpr/cond/branch_1_fun/ppermute | solution.py:473
  56.3 3.5 %collective-permute-start.36 = (f32[8,256]{1,0:T(8,128)S(1)}, f32[8,256]{1,0:T(8,128)}, u32[]{:S(2)}, u32[]{:S(2)}) collective-permute-start(f32[8,256]{1,0:T(8,128)S(1)} %get-tuple-element.783), channel_id=1, source_target_pairs={{0,192},{16,208},{32,224},{48,240},{64,0},{80,16},{96,32},{112,48}... | collective-permute-start | bytes 24584 | tf_op jit(solution)/shard_map/while/body/eval_jaxpr/cond/branch_1_fun/ppermute | solution.py:473
  61.0 13.4 %collective-permute-start.10 = (f32[168,256]{1,0:T(8,128)S(1)}, f32[168,256]{1,0:T(8,128)}, u32[]{:S(2)}, u32[]{:S(2)}) collective-permute-start(f32[168,256]{1,0:T(8,128)S(1)} %get-tuple-element.484), channel_id=1, source_target_pairs={{245,0},{246,1},{247,2},{248,3},{249,4},{250,5},{251,6},{252,7},{2... | collective-permute-start | bytes 516104 | tf_op jit(solution)/shard_map/while/body/eval_jaxpr/cond/branch_1_fun/cond/branch_1_fun/ppermute | solution.py:413
  67.6 10.1 %collective-permute-start.11 = (f32[168,256]{1,0:T(8,128)S(1)}, f32[168,256]{1,0:T(8,128)}, u32[]{:S(2)}, u32[]{:S(2)}) collective-permute-start(f32[168,256]{1,0:T(8,128)S(1)} %get-tuple-element.485), channel_id=1, source_target_pairs={{27,0},{28,1},{29,2},{30,3},{31,4},{16,5},{17,6},{18,7},{19,8},{20... | collective-permute-start | bytes 516104 | tf_op jit(solution)/shard_map/while/body/eval_jaxpr/cond/branch_1_fun/cond/branch_1_fun/ppermute | solution.py:413

commit v2 on v1

--- a/solution.py
+++ b/solution.py
@@ -256,11 +256,13 @@
     mr_ref,
     ml_ref,
     t_ref,
-    s_ref,
+    s_hbm,
     p_ref,
     q_ref,
+    s_ref,
     in_sems,
     out_sems,
+    s_sem,
 ):
     slab_rows, cells = p_ref.shape[1:3]
 
@@ -285,6 +287,8 @@
     at = lax.broadcasted_iota(jnp.int32, s_ref.shape, 1)
     x = m_x + first + jnp.where(lax.broadcasted_iota(jnp.int32, s_ref.shape, 0) == 1, second, 0.0)
     s_ref[...] = jnp.where(at == 0, rho, jnp.where(at == 1, x, jnp.where(at == 2, m_y, m_z)))
+    totals = pltpu.make_async_copy(s_ref, s_hbm, s_sem)
+    totals.start()
 
     load = streamed(p_ref, rl, rr, wu, wd, slab_rows)
 
@@ -316,6 +320,7 @@
     def _():
         all_rows(store)
 
+    totals.wait()
     for y in range(slab_rows):
         leaving(y).wait()
 
@@ -441,10 +446,13 @@
     )
     following = pl.pallas_call(
         lambda *refs: next_kernel(all_cells, *refs),
-        out_shape=(state,) + edge_outs + (near(*table), near(STEPS, 4)),
+        out_shape=(state,) + edge_outs + (near(*table), pltpu.HBM((STEPS, 4), jnp.float32)),
         in_specs=[SMEM, SMEM, HBM] + [VMEM] * 5,
-        out_specs=(HBM,) + (VMEM,) * 5,
-        scratch_shapes=buffers + row_sems,
+        out_specs=(HBM,) + (VMEM,) * 4 + (HBM,),
+        scratch_shapes=buffers
+        + [pltpu.VMEM((STEPS, 4), jnp.float32)]
+        + row_sems
+        + [pltpu.SemaphoreType.DMA],
         input_output_aliases={2: 0},
         compiler_params=PARAMS,
         name="following",

time: 83.8 us -> 75 us (0.89)
  the two profiles are of different devices: /device:TPU:1 before, /device:TPU:32 now
where the time goes in v2:
time: 75 us; the launch traced here: 74.9 us
  starting transfers between devices  33 us (44%)
  waiting for transfers between devices  20.4 us (27%)
  Pallas kernels  18.1 us (24%)
  between operations  2.24 us (3%)
    ppermute x4, waiting for transfers between devices, displaced(): return lax.ppermute(value, both, route)  14.6 us
    pallas_call x2, Pallas kernels, step(): following(at, slab, pltpu.with_memory_space_constraint(p, pltpu.HBM), *ke...  11.3 us
    ppermute x4, starting transfers between devices, displaced(): return lax.ppermute(value, both, route)  11.2 us
    ppermute x3, starting transfers between devices, apart(): lax.ppermute(value, 'slab', [(i, (i + distance) % slabs) for i in range(s...  10.4 us
    ppermute x4, starting transfers between devices, beside(): return lax.ppermute(value, 'flow', route)  7.86 us
    pallas_call x1, Pallas kernels, local(): first(pltpu.with_memory_space_constraint(populations, pltpu.HBM))  4.7 us
    all_to_all x1, waiting for transfers between devices, local(): gathered = lax.all_to_all(sums, 'flow', 0, 0)  3.85 us
    all_to_all x1, starting transfers between devices, local(): gathered = lax.all_to_all(sums, 'flow', 0, 0)  3.48 us
  transfers between devices with their start and end apart: 12, of which 6 were waited for; matrix products, arithmetic and copies ran while one was open for 1% of the time, Pallas kernels for 0%

profile of v2, /device:TPU:32, one launch (start us, length us, event | category | flops | bytes accessed | tf_op | source)
XLA Modules:
  0.0 74.9 jit_solution(7216390030633286879)
XLA Ops:
  0.6 4.7 %first.1 = (f32[19,8,32,256]{3,2,1,0:T(8,128)}, f32[10,32,256]{2,1,0:T(8,128)S(1)}, f32[208,256]{1,0:T(8,128)S(1)}, f32[208,256]{1,0:T(8,128)S(1)}, f32[16,1,128...) custom-call(f32[19,8,32,256]{3,2,1,0:T(8,128)} %f_hbm.1), custom_call_target="tpu_custom_call" | custom-call | tf_op jit(solution)/shard_map/first/pallas_call | solution.py:514
  5.4 3.8 %collective-permute-start.38 = (f32[208,256]{1,0:T(8,128)S(1)}, f32[208,256]{1,0:T(8,128)S(1)}, u32[]{:S(2)}, u32[]{:S(2)}) collective-permute-start(f32[208,256]{1,0:T(8,128)S(1)} %get-tuple-element.566), channel_id=1, source_target_pairs={{1,0},{2,1},{3,2},{4,3},{5,4},{6,5},{7,6},{8,7},{9,8},{10,9},{11,1... | collective-permute-start | bytes 638984 | tf_op jit(solution)/shard_map/ppermute | solution.py:411
  9.3 3.5 %all-to-all-start = ((f32[16,1,128]{2,1,0:T(1,128)}), f32[16,1,128]{2,1,0:T(1,128)S(1)}, u32[]{:S(2)}, u32[]{:S(2)}) async-start(f32[16,1,128]{2,1,0:T(1,128)} %get-tuple-element.571), calls=%async_computation | async-start | bytes 16384 | tf_op jit(solution)/shard_map/all_to_all | solution.py:516
  14.8 3.8 %all-to-all-done = f32[16,1,128]{2,1,0:T(1,128)S(1)} async-done(((f32[16,1,128]{2,1,0:T(1,128)}), f32[16,1,128]{2,1,0:T(1,128)S(1)}, u32[]{:S(2)}, u32[]{:S(2)}) %all-to-all-start) | async-done | bytes 8224 | tf_op jit(solution)/shard_map/all_to_all | solution.py:516
  18.6 56.1 %while.35 = (s32[]{:T(128)}, f32[19,8,32,256]{3,2,1,0:T(8,128)}, f32[10,32,256]{2,1,0:T(8,128)S(1)}, f32[208,256]{1,0:T(8,128)S(1)}, f32[208,256]{1,0:T(8,128)S(...) while((s32[]{:T(128)}, f32[19,8,32,256]{3,2,1,0:T(8,128)}, ...), condition=%wide.region_23.24_spmd, body=%wide.region_0.23_spmd.sunk | while | flops 25 | bytes 4899742 | solution.py:519
  19.9 12.2 %conditional.8 = ((f32[168,256]{1,0:T(8,128)}, f32[168,256]{1,0:T(8,128)})) conditional(s32[]{:T(128)} %clamp.23, (s32[]{:T(128)}, f32[168,256]{1,0:T(8,128)S(1)}, f32[168,256]{1,0:T(8,128)S(1)}) %tuple.127, (s32[]{:T(128)}, f32[168,256]{1,0:T(8,128)S(1)}, f32[168,256]{1,0:T(8,128)S(1)}) %tuple.127, (s32[]{:T(128)}, ...), branch_computations={%region_1.5_spmd, %region_6.10_spmd, %region_11.15_spmd, %region_1... | conditional | flops 1 | bytes 1376392 | solution.py:493
  19.9 12.2 %conditional.2 = (f32[168,256]{1,0:T(8,128)}, f32[168,256]{1,0:T(8,128)}) conditional(s32[]{:T(128)} %clamp.19, (f32[168,256]{1,0:T(8,128)S(1)}, f32[168,256]{1,0:T(8,128)S(1)}) %tuple.90, (f32[168,256]{1,0:T(8,128)S(1)}, f32[168,256]{1,0:T(8,128)S(1)}) %tuple.90, (f32[168,256]{1,0:T(8,128)S(1)}, ...), branch_computations={%region_12.11_spmd, %region_13.12_spmd, %region_14.13_spmd, %regio... | conditional | bytes 1376352 | solution.py:469
  20.0 2.7 %collective-permute-start.22 = (f32[168,256]{1,0:T(8,128)S(1)}, f32[168,256]{1,0:T(8,128)}, u32[]{:S(2)}, u32[]{:S(2)}) collective-permute-start(f32[168,256]{1,0:T(8,128)S(1)} %get-tuple-element.499), channel_id=1, source_target_pairs={{251,0},{252,1},{253,2},{254,3},{255,4},{240,5},{241,6},{242,7},{2... | collective-permute-start | bytes 516104 | tf_op jit(solution)/shard_map/while/body/eval_jaxpr/cond/branch_2_fun/cond/branch_3_fun/ppermute | solution.py:418
  22.7 3.6 %collective-permute-start.23 = (f32[168,256]{1,0:T(8,128)S(1)}, f32[168,256]{1,0:T(8,128)}, u32[]{:S(2)}, u32[]{:S(2)}) collective-permute-start(f32[168,256]{1,0:T(8,128)S(1)} %get-tuple-element.500), channel_id=1, source_target_pairs={{21,0},{22,1},{23,2},{24,3},{25,4},{26,5},{27,6},{28,7},{29,8},{30... | collective-permute-start | bytes 516104 | tf_op jit(solution)/shard_map/while/body/eval_jaxpr/cond/branch_2_fun/cond/branch_3_fun/ppermute | solution.py:418
  26.3 5.8 %collective-permute-done.22 = f32[168,256]{1,0:T(8,128)} collective-permute-done((f32[168,256]{1,0:T(8,128)S(1)}, f32[168,256]{1,0:T(8,128)}, u32[]{:S(2)}, u32[]{:S(2)}) %collective-permute-start.22) | collective-permute-done | bytes 172064 | tf_op jit(solution)/shard_map/while/body/eval_jaxpr/cond/branch_2_fun/cond/branch_3_fun/ppermute | solution.py:418
  32.1 6.4 %following.8 = (f32[19,8,32,256]{3,2,1,0:T(8,128)}, f32[10,32,256]{2,1,0:T(8,128)S(1)}, f32[208,256]{1,0:T(8,128)S(1)}, f32[208,256]{1,0:T(8,128)S(1)}, f32[8,256]{1,0:T(8,128)S(1)}, /*index=5*/f32[2,4]{1,0:T(2,128)}) custom-call(s32[1]{0:T(128)} %bitcast.5.step_ref.refs_0_, s32[1]{0:T(128)} %get-tuple-element.843.slab_ref.refs_1_, ...), custom_call_target="tpu_custom_call", output_to_operand_aliasing={{0}: (2, {})} | custom-call | tf_op jit(solution)/shard_map/while/body/eval_jaxpr/following/pallas_call | solution.py:494
  38.5 16.4 %conditional.9 = ((f32[208,256]{1,0:T(8,128)S(1)}, f32[208,256]{1,0:T(8,128)S(1)}, f32[8,256]{1,0:T(8,128)S(1)}, f32[8,256]{1,0:T(8,128)}, f32[8,256]{1,0:T(8,128)}, /*index=5*/f32[8,256]{1,0:T(8,128)})) conditional(s32[]{:T(128)} %convert_element_type.11, (f32[208,256]{1,0:T(8,128)S(1)}, f32[208,256]{1,0:T(8,128)S(1)}, f32[8,256]{1,0:T(8,128)S(1)}, ...), branch_computations={%region_21.21_spmd, %region_22.22_spmd} | conditional | bytes 2670848 | solution.py:500
  38.5 1.1 %collective-permute-start.32 = (f32[208,256]{1,0:T(8,128)S(1)}, f32[208,256]{1,0:T(8,128)S(1)}, u32[]{:S(2)}, u32[]{:S(2)}) collective-permute-start(f32[208,256]{1,0:T(8,128)S(1)} %get-tuple-element.515), channel_id=1, source_target_pairs={{15,0},{0,1},{1,2},{2,3},{3,4},{4,5},{5,6},{6,7},{7,8},{8,9},{9,10... | collective-permute-start | bytes 638984 | tf_op jit(solution)/shard_map/while/body/eval_jaxpr/cond/branch_1_fun/ppermute | solution.py:411
  39.6 2.8 %collective-permute-start.33 = (f32[208,256]{1,0:T(8,128)S(1)}, f32[208,256]{1,0:T(8,128)S(1)}, u32[]{:S(2)}, u32[]{:S(2)}) collective-permute-start(f32[208,256]{1,0:T(8,128)S(1)} %get-tuple-element.516), channel_id=1, source_target_pairs={{1,0},{2,1},{3,2},{4,3},{5,4},{6,5},{7,6},{8,7},{9,8},{10,9},{11,1... | collective-permute-start | bytes 638984 | tf_op jit(solution)/shard_map/while/body/eval_jaxpr/cond/branch_1_fun/ppermute | solution.py:411
  42.5 3.3 %collective-permute-start.34 = (f32[8,256]{1,0:T(8,128)S(1)}, f32[8,256]{1,0:T(8,128)}, u32[]{:S(2)}, u32[]{:S(2)}) collective-permute-start(f32[8,256]{1,0:T(8,128)S(1)} %get-tuple-element.783), channel_id=1, source_target_pairs={{0,64},{16,80},{32,96},{48,112},{64,128},{80,144},{96,160},{112,17... | collective-permute-start | bytes 24584 | tf_op jit(solution)/shard_map/while/body/eval_jaxpr/cond/branch_1_fun/ppermute | solution.py:481
  45.7 4.5 %collective-permute-start.35 = (f32[8,256]{1,0:T(8,128)S(1)}, f32[8,256]{1,0:T(8,128)}, u32[]{:S(2)}, u32[]{:S(2)}) collective-permute-start(f32[8,256]{1,0:T(8,128)S(1)} %get-tuple-element.783), channel_id=1, source_target_pairs={{0,128},{16,144},{32,160},{48,176},{64,192},{80,208},{96,224},{112... | collective-permute-start | bytes 24584 | tf_op jit(solution)/shard_map/while/body/eval_jaxpr/cond/branch_1_fun/ppermute | solution.py:481
  50.2 2.7 %collective-permute-start.36 = (f32[8,256]{1,0:T(8,128)S(1)}, f32[8,256]{1,0:T(8,128)}, u32[]{:S(2)}, u32[]{:S(2)}) collective-permute-start(f32[8,256]{1,0:T(8,128)S(1)} %get-tuple-element.783), channel_id=1, source_target_pairs={{0,192},{16,208},{32,224},{48,240},{64,0},{80,16},{96,32},{112,48}... | collective-permute-start | bytes 24584 | tf_op jit(solution)/shard_map/while/body/eval_jaxpr/cond/branch_1_fun/ppermute | solution.py:481
  53.4 1.5 %collective-permute-done.36 = f32[8,256]{1,0:T(8,128)} collective-permute-done((f32[8,256]{1,0:T(8,128)S(1)}, f32[8,256]{1,0:T(8,128)}, u32[]{:S(2)}, u32[]{:S(2)}) %collective-permute-start.36) | collective-permute-done | bytes 8224 | tf_op jit(solution)/shard_map/while/body/eval_jaxpr/cond/branch_1_fun/ppermute | solution.py:481
  56.0 13.7 %conditional.8 = ((f32[168,256]{1,0:T(8,128)}, f32[168,256]{1,0:T(8,128)})) conditional(s32[]{:T(128)} %clamp.23, (s32[]{:T(128)}, f32[168,256]{1,0:T(8,128)S(1)}, f32[168,256]{1,0:T(8,128)S(1)}) %tuple.127, (s32[]{:T(128)}, f32[168,256]{1,0:T(8,128)S(1)}, f32[168,256]{1,0:T(8,128)S(1)}) %tuple.127, (s32[]{:T(128)}, ...), branch_computations={%region_1.5_spmd, %region_6.10_spmd, %region_11.15_spmd, %region_1... | conditional | flops 1 | bytes 1376392 | solution.py:493
  56.0 13.7 %conditional = (f32[168,256]{1,0:T(8,128)}, f32[168,256]{1,0:T(8,128)}) conditional(s32[]{:T(128)} %clamp.17, (f32[168,256]{1,0:T(8,128)S(1)}, f32[168,256]{1,0:T(8,128)S(1)}) %tuple.74, (f32[168,256]{1,0:T(8,128)S(1)}, f32[168,256]{1,0:T(8,128)S(1)}) %tuple.74, (f32[168,256]{1,0:T(8,128)S(1)}, ...), branch_computations={%region_2.1_spmd, %region_3.2_spmd, %region_4.3_spmd, %region_5.4_... | conditional | bytes 1376352 | solution.py:469
  56.1 4.9 %collective-permute-start.4 = (f32[168,256]{1,0:T(8,128)S(1)}, f32[168,256]{1,0:T(8,128)}, u32[]{:S(2)}, u32[]{:S(2)}) collective-permute-start(f32[168,256]{1,0:T(8,128)S(1)} %get-tuple-element.475), channel_id=1, source_target_pairs={{242,0},{243,1},{244,2},{245,3},{246,4},{247,5},{248,6},{249,7},{2... | collective-permute-start | bytes 516104 | tf_op jit(solution)/shard_map/while/body/eval_jaxpr/cond/branch_0_fun/cond/branch_2_fun/ppermute | solution.py:418
  60.9 4.9 %collective-permute-done.4 = f32[168,256]{1,0:T(8,128)} collective-permute-done((f32[168,256]{1,0:T(8,128)S(1)}, f32[168,256]{1,0:T(8,128)}, u32[]{:S(2)}, u32[]{:S(2)}) %collective-permute-start.4) | collective-permute-done | bytes 172064 | tf_op jit(solution)/shard_map/while/body/eval_jaxpr/cond/branch_0_fun/cond/branch_2_fun/ppermute | solution.py:418
  65.9 3.9 %collective-permute-done.5 = f32[168,256]{1,0:T(8,128)} collective-permute-done((f32[168,256]{1,0:T(8,128)S(1)}, f32[168,256]{1,0:T(8,128)}, u32[]{:S(2)}, u32[]{:S(2)}) %collective-permute-start.5) | collective-permute-done | bytes 172064 | tf_op jit(solution)/shard_map/while/body/eval_jaxpr/cond/branch_0_fun/cond/branch_2_fun/ppermute | solution.py:418
  69.8 4.9 %following.8 = (f32[19,8,32,256]{3,2,1,0:T(8,128)}, f32[10,32,256]{2,1,0:T(8,128)S(1)}, f32[208,256]{1,0:T(8,128)S(1)}, f32[208,256]{1,0:T(8,128)S(1)}, f32[8,256]{1,0:T(8,128)S(1)}, /*index=5*/f32[2,4]{1,0:T(2,128)}) custom-call(s32[1]{0:T(128)} %bitcast.5.step_ref.refs_0_, s32[1]{0:T(128)} %get-tuple-element.843.slab_ref.refs_1_, ...), custom_call_target="tpu_custom_call", output_to_operand_aliasing={{0}: (2, {})} | custom-call | tf_op jit(solution)/shard_map/while/body/eval_jaxpr/following/pallas_call | solution.py:494
  (25 shorter events, 3.3 us)
Async XLA Ops:
  0.6 12.1 %copy-start = (s32[2]{0:T(128)S(1)}, s32[2]{0:T(128)}, u32[]{:S(2)}) copy-start(s32[2]{0:T(128)} %param.28) | copy-start | bytes 28
  0.6 18.0 %copy-start.1 = (s32[2]{0:T(128)S(1)}, s32[2]{0:T(128)}, u32[]{:S(2)}) copy-start(s32[2]{0:T(128)} %param.29) | copy-start | bytes 28
  5.4 13.3 %collective-permute-start.37 = (f32[208,256]{1,0:T(8,128)S(1)}, f32[208,256]{1,0:T(8,128)S(1)}, u32[]{:S(2)}, u32[]{:S(2)}) collective-permute-start(f32[208,256]{1,0:T(8,128)S(1)} %get-tuple-element.565), channel_id=1, source_target_pairs={{15,0},{0,1},{1,2},{2,3},{3,4},{4,5},{5,6},{6,7},{7,8},{8,9},{9,10... | collective-permute-start | bytes 638984 | tf_op jit(solution)/shard_map/ppermute | solution.py:411
  5.4 13.2 %collective-permute-start.38 = (f32[208,256]{1,0:T(8,128)S(1)}, f32[208,256]{1,0:T(8,128)S(1)}, u32[]{:S(2)}, u32[]{:S(2)}) collective-permute-start(f32[208,256]{1,0:T(8,128)S(1)} %get-tuple-element.566), channel_id=1, source_target_pairs={{1,0},{2,1},{3,2},{4,3},{5,4},{6,5},{7,6},{8,7},{9,8},{10,9},{11,1... | collective-permute-start | bytes 638984 | tf_op jit(solution)/shard_map/ppermute | solution.py:411
  9.3 9.3 %all-to-all-start = ((f32[16,1,128]{2,1,0:T(1,128)}), f32[16,1,128]{2,1,0:T(1,128)S(1)}, u32[]{:S(2)}, u32[]{:S(2)}) async-start(f32[16,1,128]{2,1,0:T(1,128)} %get-tuple-element.571), calls=%async_computation | async-start | bytes 16384 | tf_op jit(solution)/shard_map/all_to_all | solution.py:516
  20.0 12.1 %collective-permute-start.22 = (f32[168,256]{1,0:T(8,128)S(1)}, f32[168,256]{1,0:T(8,128)}, u32[]{:S(2)}, u32[]{:S(2)}) collective-permute-start(f32[168,256]{1,0:T(8,128)S(1)} %get-tuple-element.499), channel_id=1, source_target_pairs={{251,0},{252,1},{253,2},{254,3},{255,4},{240,5},{241,6},{242,7},{2... | collective-permute-start | bytes 516104 | tf_op jit(solution)/shard_map/while/body/eval_jaxpr/cond/branch_2_fun/cond/branch_3_fun/ppermute | solution.py:418
  22.7 9.4 %collective-permute-start.23 = (f32[168,256]{1,0:T(8,128)S(1)}, f32[168,256]{1,0:T(8,128)}, u32[]{:S(2)}, u32[]{:S(2)}) collective-permute-start(f32[168,256]{1,0:T(8,128)S(1)} %get-tuple-element.500), channel_id=1, source_target_pairs={{21,0},{22,1},{23,2},{24,3},{25,4},{26,5},{27,6},{28,7},{29,8},{30... | collective-permute-start | bytes 516104 | tf_op jit(solution)/shard_map/while/body/eval_jaxpr/cond/branch_2_fun/cond/branch_3_fun/ppermute | solution.py:418
  38.5 14.4 %collective-permute-start.32 = (f32[208,256]{1,0:T(8,128)S(1)}, f32[208,256]{1,0:T(8,128)S(1)}, u32[]{:S(2)}, u32[]{:S(2)}) collective-permute-start(f32[208,256]{1,0:T(8,128)S(1)} %get-tuple-element.515), channel_id=1, source_target_pairs={{15,0},{0,1},{1,2},{2,3},{3,4},{4,5},{5,6},{6,7},{7,8},{8,9},{9,10... | collective-permute-start | bytes 638984 | tf_op jit(solution)/shard_map/while/body/eval_jaxpr/cond/branch_1_fun/ppermute | solution.py:411
  39.6 13.3 %collective-permute-start.33 = (f32[208,256]{1,0:T(8,128)S(1)}, f32[208,256]{1,0:T(8,128)S(1)}, u32[]{:S(2)}, u32[]{:S(2)}) collective-permute-start(f32[208,256]{1,0:T(8,128)S(1)} %get-tuple-element.516), channel_id=1, source_target_pairs={{1,0},{2,1},{3,2},{4,3},{5,4},{6,5},{7,6},{8,7},{9,8},{10,9},{11,1... | collective-permute-start | bytes 638984 | tf_op jit(solution)/shard_map/while/body/eval_jaxpr/cond/branch_1_fun/ppermute | solution.py:411
  42.5 10.5 %collective-permute-start.34 = (f32[8,256]{1,0:T(8,128)S(1)}, f32[8,256]{1,0:T(8,128)}, u32[]{:S(2)}, u32[]{:S(2)}) collective-permute-start(f32[8,256]{1,0:T(8,128)S(1)} %get-tuple-element.783), channel_id=1, source_target_pairs={{0,64},{16,80},{32,96},{48,112},{64,128},{80,144},{96,160},{112,17... | collective-permute-start | bytes 24584 | tf_op jit(solution)/shard_map/while/body/eval_jaxpr/cond/branch_1_fun/ppermute | solution.py:481
  45.7 7.7 %collective-permute-start.35 = (f32[8,256]{1,0:T(8,128)S(1)}, f32[8,256]{1,0:T(8,128)}, u32[]{:S(2)}, u32[]{:S(2)}) collective-permute-start(f32[8,256]{1,0:T(8,128)S(1)} %get-tuple-element.783), channel_id=1, source_target_pairs={{0,128},{16,144},{32,160},{48,176},{64,192},{80,208},{96,224},{112... | collective-permute-start | bytes 24584 | tf_op jit(solution)/shard_map/while/body/eval_jaxpr/cond/branch_1_fun/ppermute | solution.py:481
  50.2 4.7 %collective-permute-start.36 = (f32[8,256]{1,0:T(8,128)S(1)}, f32[8,256]{1,0:T(8,128)}, u32[]{:S(2)}, u32[]{:S(2)}) collective-permute-start(f32[8,256]{1,0:T(8,128)S(1)} %get-tuple-element.783), channel_id=1, source_target_pairs={{0,192},{16,208},{32,224},{48,240},{64,0},{80,16},{96,32},{112,48}... | collective-permute-start | bytes 24584 | tf_op jit(solution)/shard_map/while/body/eval_jaxpr/cond/branch_1_fun/ppermute | solution.py:481
  56.1 9.8 %collective-permute-start.4 = (f32[168,256]{1,0:T(8,128)S(1)}, f32[168,256]{1,0:T(8,128)}, u32[]{:S(2)}, u32[]{:S(2)}) collective-permute-start(f32[168,256]{1,0:T(8,128)S(1)} %get-tuple-element.475), channel_id=1, source_target_pairs={{242,0},{243,1},{244,2},{245,3},{246,4},{247,5},{248,6},{249,7},{2... | collective-permute-start | bytes 516104 | tf_op jit(solution)/shard_map/while/body/eval_jaxpr/cond/branch_0_fun/cond/branch_2_fun/ppermute | solution.py:418
  60.9 8.8 %collective-permute-start.5 = (f32[168,256]{1,0:T(8,128)S(1)}, f32[168,256]{1,0:T(8,128)}, u32[]{:S(2)}, u32[]{:S(2)}) collective-permute-start(f32[168,256]{1,0:T(8,128)S(1)} %get-tuple-element.476), channel_id=1, source_target_pairs={{30,0},{31,1},{16,2},{17,3},{18,4},{19,5},{20,6},{21,7},{22,8},{23... | collective-permute-start | bytes 516104 | tf_op jit(solution)/shard_map/while/body/eval_jaxpr/cond/branch_0_fun/cond/branch_2_fun/ppermute | solution.py:418

commit v3 on v2

--- a/solution.py
+++ b/solution.py
@@ -376,9 +376,8 @@
         else:
             start, out = own - c_x - r - 1, down_ref
             low, high = a, 1.0 - a
-        line = s_ref[...]
-        count = line.shape[0]
-        line = low * line + high * pltpu.roll(line, count - 1, axis=0)
+        count = cells + 2 * REACH + 16
+        line = low * s_ref[0:count, :] + high * s_ref[1 : count + 1, :]
         at = (j % 5) * cells
         out[at : at + cells, :] = pltpu.roll(line, count - start, axis=0)[:cells]
 
@@ -440,7 +439,7 @@
         out_shape=(near(*side), near(*side)),
         in_specs=[SMEM] * 4 + [VMEM] * 8,
         out_specs=(VMEM,) * 2,
-        scratch_shapes=[pltpu.VMEM((cells + 2 * REACH + 16, depth), jnp.float32)],
+        scratch_shapes=[pltpu.VMEM((cells + 2 * REACH + 24, depth), jnp.float32)],
         compiler_params=PARAMS,
         name="walls",
     )

time: 75 us -> 83.4 us (1.11)
  the two profiles are of different devices: /device:TPU:32 before, /device:TPU:1 now
where the time goes in v3:
time: 83.4 us; the launch traced here: 82.6 us
  starting transfers between devices  45.1 us (54%)
  Pallas kernels  18.1 us (22%)
  waiting for transfers between devices  16 us (19%)
  between operations  2.22 us (3%)
    ppermute x4, starting transfers between devices, displaced(): return lax.ppermute(value, both, route)  22.1 us
    ppermute x4, waiting for transfers between devices, displaced(): return lax.ppermute(value, both, route)  11.7 us
    pallas_call x2, Pallas kernels, step(): following(at, slab, pltpu.with_memory_space_constraint(p, pltpu.HBM), *ke...  11.3 us
    ppermute x3, starting transfers between devices, apart(): lax.ppermute(value, 'slab', [(i, (i + distance) % slabs) for i in range(s...  9.54 us
    all_to_all x1, starting transfers between devices, local(): gathered = lax.all_to_all(sums, 'flow', 0, 0)  7.03 us
    ppermute x4, starting transfers between devices, beside(): return lax.ppermute(value, 'flow', route)  6.39 us
    pallas_call x1, Pallas kernels, local(): first(pltpu.with_memory_space_constraint(populations, pltpu.HBM))  4.7 us
    all_to_all x1, waiting for transfers between devices, local(): gathered = lax.all_to_all(sums, 'flow', 0, 0)  3.55 us
  transfers between devices with their start and end apart: 12, of which 4 were waited for; matrix products, arithmetic and copies ran while one was open for 1% of the time, Pallas kernels for 0%

profile of v3, /device:TPU:1, one launch (start us, length us, event | category | flops | bytes accessed | tf_op | source)
XLA Modules:
  0.0 82.6 jit_solution(4669072754245470413)
XLA Ops:
  0.6 4.7 %first.1 = (f32[19,8,32,256]{3,2,1,0:T(8,128)}, f32[10,32,256]{2,1,0:T(8,128)S(1)}, f32[208,256]{1,0:T(8,128)S(1)}, f32[208,256]{1,0:T(8,128)S(1)}, f32[16,1,128...) custom-call(f32[19,8,32,256]{3,2,1,0:T(8,128)} %f_hbm.1), custom_call_target="tpu_custom_call" | custom-call | tf_op jit(solution)/shard_map/first/pallas_call | solution.py:513
  5.4 2.7 %collective-permute-start.37 = (f32[208,256]{1,0:T(8,128)S(1)}, f32[208,256]{1,0:T(8,128)S(1)}, u32[]{:S(2)}, u32[]{:S(2)}) collective-permute-start(f32[208,256]{1,0:T(8,128)S(1)} %get-tuple-element.565), channel_id=1, source_target_pairs={{15,0},{0,1},{1,2},{2,3},{3,4},{4,5},{5,6},{6,7},{7,8},{8,9},{9,10... | collective-permute-start | bytes 638984 | tf_op jit(solution)/shard_map/ppermute | solution.py:410
  8.0 0.7 collective-permute-start.38
  8.8 7.0 %all-to-all-start = ((f32[16,1,128]{2,1,0:T(1,128)}), f32[16,1,128]{2,1,0:T(1,128)S(1)}, u32[]{:S(2)}, u32[]{:S(2)}) async-start(f32[16,1,128]{2,1,0:T(1,128)} %get-tuple-element.571), calls=%async_computation | async-start | bytes 16384 | tf_op jit(solution)/shard_map/all_to_all | solution.py:515
  17.8 3.6 %all-to-all-done = f32[16,1,128]{2,1,0:T(1,128)S(1)} async-done(((f32[16,1,128]{2,1,0:T(1,128)}), f32[16,1,128]{2,1,0:T(1,128)S(1)}, u32[]{:S(2)}, u32[]{:S(2)}) %all-to-all-start) | async-done | bytes 8224 | tf_op jit(solution)/shard_map/all_to_all | solution.py:515
  21.3 61.1 %while.35 = (s32[]{:T(128)}, f32[19,8,32,256]{3,2,1,0:T(8,128)}, f32[10,32,256]{2,1,0:T(8,128)S(1)}, f32[208,256]{1,0:T(8,128)S(1)}, f32[208,256]{1,0:T(8,128)S(...) while((s32[]{:T(128)}, f32[19,8,32,256]{3,2,1,0:T(8,128)}, ...), condition=%wide.region_23.24_spmd, body=%wide.region_0.23_spmd.sunk | while | flops 25 | bytes 4899742 | solution.py:518
  21.6 1.0 %walls.8 = (f32[168,256]{1,0:T(8,128)S(1)}, f32[168,256]{1,0:T(8,128)S(1)}) custom-call(s32[1]{0:T(128)} %bitcast.5.step_ref.refs_0_, s32[1]{0:T(128)} %get-tuple-element.843.slab_ref.refs_1_, s32[2]{0:T(128)S(1)} %get-tuple-element.844.d_ref, s32[2]{0:T(128)S(1)} %get-tuple-element.845.n_ref, f32[16,1,128]{2,1,0:T(1,128)S(1)} %get-tuple-element.846.g_ref, ...), custom_call_target="tpu_custom_call" | custom-call | tf_op jit(solution)/shard_map/while/body/eval_jaxpr/walls/pallas_call | solution.py:485
  22.6 11.4 %conditional.8 = ((f32[168,256]{1,0:T(8,128)}, f32[168,256]{1,0:T(8,128)})) conditional(s32[]{:T(128)} %clamp.23, (s32[]{:T(128)}, f32[168,256]{1,0:T(8,128)S(1)}, f32[168,256]{1,0:T(8,128)S(1)}) %tuple.127, (s32[]{:T(128)}, f32[168,256]{1,0:T(8,128)S(1)}, f32[168,256]{1,0:T(8,128)S(1)}) %tuple.127, (s32[]{:T(128)}, ...), branch_computations={%region_1.5_spmd, %region_6.10_spmd, %region_11.15_spmd, %region_1... | conditional | flops 1 | bytes 1376392 | solution.py:492
  22.7 11.4 %conditional.2 = (f32[168,256]{1,0:T(8,128)}, f32[168,256]{1,0:T(8,128)}) conditional(s32[]{:T(128)} %clamp.19, (f32[168,256]{1,0:T(8,128)S(1)}, f32[168,256]{1,0:T(8,128)S(1)}) %tuple.90, (f32[168,256]{1,0:T(8,128)S(1)}, f32[168,256]{1,0:T(8,128)S(1)}) %tuple.90, (f32[168,256]{1,0:T(8,128)S(1)}, ...), branch_computations={%region_12.11_spmd, %region_13.12_spmd, %region_14.13_spmd, %regio... | conditional | bytes 1376352 | solution.py:468
  22.9 7.1 %collective-permute-start.21 = (f32[168,256]{1,0:T(8,128)S(1)}, f32[168,256]{1,0:T(8,128)}, u32[]{:S(2)}, u32[]{:S(2)}) collective-permute-start(f32[168,256]{1,0:T(8,128)S(1)} %get-tuple-element.498), channel_id=1, source_target_pairs={{22,0},{23,1},{24,2},{25,3},{26,4},{27,5},{28,6},{29,7},{30,8},{31... | collective-permute-start | bytes 516104 | tf_op jit(solution)/shard_map/while/body/eval_jaxpr/cond/branch_2_fun/cond/branch_2_fun/ppermute | solution.py:417
  29.9 4.1 %collective-permute-done.20 = f32[168,256]{1,0:T(8,128)} collective-permute-done((f32[168,256]{1,0:T(8,128)S(1)}, f32[168,256]{1,0:T(8,128)}, u32[]{:S(2)}, u32[]{:S(2)}) %collective-permute-start.20) | collective-permute-done | bytes 172064 | tf_op jit(solution)/shard_map/while/body/eval_jaxpr/cond/branch_2_fun/cond/branch_2_fun/ppermute | solution.py:417
  34.0 6.4 %following.8 = (f32[19,8,32,256]{3,2,1,0:T(8,128)}, f32[10,32,256]{2,1,0:T(8,128)S(1)}, f32[208,256]{1,0:T(8,128)S(1)}, f32[208,256]{1,0:T(8,128)S(1)}, f32[8,256]{1,0:T(8,128)S(1)}, /*index=5*/f32[2,4]{1,0:T(2,128)}) custom-call(s32[1]{0:T(128)} %bitcast.5.step_ref.refs_0_, s32[1]{0:T(128)} %get-tuple-element.843.slab_ref.refs_1_, ...), custom_call_target="tpu_custom_call", output_to_operand_aliasing={{0}: (2, {})} | custom-call | tf_op jit(solution)/shard_map/while/body/eval_jaxpr/following/pallas_call | solution.py:493
  40.5 13.3 %conditional.9 = ((f32[208,256]{1,0:T(8,128)S(1)}, f32[208,256]{1,0:T(8,128)S(1)}, f32[8,256]{1,0:T(8,128)S(1)}, f32[8,256]{1,0:T(8,128)}, f32[8,256]{1,0:T(8,128)}, /*index=5*/f32[8,256]{1,0:T(8,128)})) conditional(s32[]{:T(128)} %convert_element_type.11, (f32[208,256]{1,0:T(8,128)S(1)}, f32[208,256]{1,0:T(8,128)S(1)}, f32[8,256]{1,0:T(8,128)S(1)}, ...), branch_computations={%region_21.21_spmd, %region_22.22_spmd} | conditional | bytes 2670848 | solution.py:499
  40.5 3.0 %collective-permute-start.32 = (f32[208,256]{1,0:T(8,128)S(1)}, f32[208,256]{1,0:T(8,128)S(1)}, u32[]{:S(2)}, u32[]{:S(2)}) collective-permute-start(f32[208,256]{1,0:T(8,128)S(1)} %get-tuple-element.515), channel_id=1, source_target_pairs={{15,0},{0,1},{1,2},{2,3},{3,4},{4,5},{5,6},{6,7},{7,8},{8,9},{9,10... | collective-permute-start | bytes 638984 | tf_op jit(solution)/shard_map/while/body/eval_jaxpr/cond/branch_1_fun/ppermute | solution.py:410
  43.5 0.8 %collective-permute-start.34 = (f32[8,256]{1,0:T(8,128)S(1)}, f32[8,256]{1,0:T(8,128)}, u32[]{:S(2)}, u32[]{:S(2)}) collective-permute-start(f32[8,256]{1,0:T(8,128)S(1)} %get-tuple-element.783), channel_id=1, source_target_pairs={{0,64},{16,80},{32,96},{48,112},{64,128},{80,144},{96,160},{112,17... | collective-permute-start | bytes 24584 | tf_op jit(solution)/shard_map/while/body/eval_jaxpr/cond/branch_1_fun/ppermute | solution.py:480
  44.3 5.1 %collective-permute-start.35 = (f32[8,256]{1,0:T(8,128)S(1)}, f32[8,256]{1,0:T(8,128)}, u32[]{:S(2)}, u32[]{:S(2)}) collective-permute-start(f32[8,256]{1,0:T(8,128)S(1)} %get-tuple-element.783), channel_id=1, source_target_pairs={{0,128},{16,144},{32,160},{48,176},{64,192},{80,208},{96,224},{112... | collective-permute-start | bytes 24584 | tf_op jit(solution)/shard_map/while/body/eval_jaxpr/cond/branch_1_fun/ppermute | solution.py:480
  49.4 3.6 %collective-permute-start.36 = (f32[8,256]{1,0:T(8,128)S(1)}, f32[8,256]{1,0:T(8,128)}, u32[]{:S(2)}, u32[]{:S(2)}) collective-permute-start(f32[8,256]{1,0:T(8,128)S(1)} %get-tuple-element.783), channel_id=1, source_target_pairs={{0,192},{16,208},{32,224},{48,240},{64,0},{80,16},{96,32},{112,48}... | collective-permute-start | bytes 24584 | tf_op jit(solution)/shard_map/while/body/eval_jaxpr/cond/branch_1_fun/ppermute | solution.py:480
  53.9 1.0 %walls.8 = (f32[168,256]{1,0:T(8,128)S(1)}, f32[168,256]{1,0:T(8,128)S(1)}) custom-call(s32[1]{0:T(128)} %bitcast.5.step_ref.refs_0_, s32[1]{0:T(128)} %get-tuple-element.843.slab_ref.refs_1_, s32[2]{0:T(128)S(1)} %get-tuple-element.844.d_ref, s32[2]{0:T(128)S(1)} %get-tuple-element.845.n_ref, f32[16,1,128]{2,1,0:T(1,128)S(1)} %get-tuple-element.846.g_ref, ...), custom_call_target="tpu_custom_call" | custom-call | tf_op jit(solution)/shard_map/while/body/eval_jaxpr/walls/pallas_call | solution.py:485
  54.9 22.5 %conditional.8 = ((f32[168,256]{1,0:T(8,128)}, f32[168,256]{1,0:T(8,128)})) conditional(s32[]{:T(128)} %clamp.23, (s32[]{:T(128)}, f32[168,256]{1,0:T(8,128)S(1)}, f32[168,256]{1,0:T(8,128)S(1)}) %tuple.127, (s32[]{:T(128)}, f32[168,256]{1,0:T(8,128)S(1)}, f32[168,256]{1,0:T(8,128)S(1)}) %tuple.127, (s32[]{:T(128)}, ...), branch_computations={%region_1.5_spmd, %region_6.10_spmd, %region_11.15_spmd, %region_1... | conditional | flops 1 | bytes 1376392 | solution.py:492
  55.0 22.5 %conditional.3 = (f32[168,256]{1,0:T(8,128)}, f32[168,256]{1,0:T(8,128)}) conditional(s32[]{:T(128)} %clamp.20, (f32[168,256]{1,0:T(8,128)S(1)}, f32[168,256]{1,0:T(8,128)S(1)}) %tuple.98, (f32[168,256]{1,0:T(8,128)S(1)}, f32[168,256]{1,0:T(8,128)S(1)}) %tuple.98, (f32[168,256]{1,0:T(8,128)S(1)}, ...), branch_computations={%region_17.16_spmd, %region_18.17_spmd, %region_19.18_spmd, %regio... | conditional | bytes 1376352 | solution.py:468
  55.0 4.5 %collective-permute-start.30 = (f32[168,256]{1,0:T(8,128)S(1)}, f32[168,256]{1,0:T(8,128)}, u32[]{:S(2)}, u32[]{:S(2)}) collective-permute-start(f32[168,256]{1,0:T(8,128)S(1)} %get-tuple-element.510), channel_id=1, source_target_pairs={{255,0},{240,1},{241,2},{242,3},{243,4},{244,5},{245,6},{246,7},{2... | collective-permute-start | bytes 516104 | tf_op jit(solution)/shard_map/while/body/eval_jaxpr/cond/branch_3_fun/cond/branch_3_fun/ppermute | solution.py:417
  59.5 10.3 %collective-permute-start.31 = (f32[168,256]{1,0:T(8,128)S(1)}, f32[168,256]{1,0:T(8,128)}, u32[]{:S(2)}, u32[]{:S(2)}) collective-permute-start(f32[168,256]{1,0:T(8,128)S(1)} %get-tuple-element.511), channel_id=1, source_target_pairs={{17,0},{18,1},{19,2},{20,3},{21,4},{22,5},{23,6},{24,7},{25,8},{26... | collective-permute-start | bytes 516104 | tf_op jit(solution)/shard_map/while/body/eval_jaxpr/cond/branch_3_fun/cond/branch_3_fun/ppermute | solution.py:417
  69.8 7.6 %collective-permute-done.31 = f32[168,256]{1,0:T(8,128)} collective-permute-done((f32[168,256]{1,0:T(8,128)S(1)}, f32[168,256]{1,0:T(8,128)}, u32[]{:S(2)}, u32[]{:S(2)}) %collective-permute-start.31) | collective-permute-done | bytes 172064 | tf_op jit(solution)/shard_map/while/body/eval_jaxpr/cond/branch_3_fun/cond/branch_3_fun/ppermute | solution.py:417
  77.5 4.9 %following.8 = (f32[19,8,32,256]{3,2,1,0:T(8,128)}, f32[10,32,256]{2,1,0:T(8,128)S(1)}, f32[208,256]{1,0:T(8,128)S(1)}, f32[208,256]{1,0:T(8,128)S(1)}, f32[8,256]{1,0:T(8,128)S(1)}, /*index=5*/f32[2,4]{1,0:T(2,128)}) custom-call(s32[1]{0:T(128)} %bitcast.5.step_ref.refs_0_, s32[1]{0:T(128)} %get-tuple-element.843.slab_ref.refs_1_, ...), custom_call_target="tpu_custom_call", output_to_operand_aliasing={{0}: (2, {})} | custom-call | tf_op jit(solution)/shard_map/while/body/eval_jaxpr/following/pallas_call | solution.py:493
  (25 shorter events, 1.7 us)
Async XLA Ops:
  0.6 15.2 %copy-start = (s32[2]{0:T(128)S(1)}, s32[2]{0:T(128)}, u32[]{:S(2)}) copy-start(s32[2]{0:T(128)} %param.28) | copy-start | bytes 28
  0.6 20.7 %copy-start.1 = (s32[2]{0:T(128)S(1)}, s32[2]{0:T(128)}, u32[]{:S(2)}) copy-start(s32[2]{0:T(128)} %param.29) | copy-start | bytes 28
  5.4 16.0 %collective-permute-start.37 = (f32[208,256]{1,0:T(8,128)S(1)}, f32[208,256]{1,0:T(8,128)S(1)}, u32[]{:S(2)}, u32[]{:S(2)}) collective-permute-start(f32[208,256]{1,0:T(8,128)S(1)} %get-tuple-element.565), channel_id=1, source_target_pairs={{15,0},{0,1},{1,2},{2,3},{3,4},{4,5},{5,6},{6,7},{7,8},{8,9},{9,10... | collective-permute-start | bytes 638984 | tf_op jit(solution)/shard_map/ppermute | solution.py:410
  8.0 13.3 %collective-permute-start.38 = (f32[208,256]{1,0:T(8,128)S(1)}, f32[208,256]{1,0:T(8,128)S(1)}, u32[]{:S(2)}, u32[]{:S(2)}) collective-permute-start(f32[208,256]{1,0:T(8,128)S(1)} %get-tuple-element.566), channel_id=1, source_target_pairs={{1,0},{2,1},{3,2},{4,3},{5,4},{6,5},{7,6},{8,7},{9,8},{10,9},{11,1... | collective-permute-start | bytes 638984 | tf_op jit(solution)/shard_map/ppermute | solution.py:410
  8.8 12.6 %all-to-all-start = ((f32[16,1,128]{2,1,0:T(1,128)}), f32[16,1,128]{2,1,0:T(1,128)S(1)}, u32[]{:S(2)}, u32[]{:S(2)}) async-start(f32[16,1,128]{2,1,0:T(1,128)} %get-tuple-element.571), calls=%async_computation | async-start | bytes 16384 | tf_op jit(solution)/shard_map/all_to_all | solution.py:515
  22.7 11.4 %collective-permute-start.20 = (f32[168,256]{1,0:T(8,128)S(1)}, f32[168,256]{1,0:T(8,128)}, u32[]{:S(2)}, u32[]{:S(2)}) collective-permute-start(f32[168,256]{1,0:T(8,128)S(1)} %get-tuple-element.497), channel_id=1, source_target_pairs={{250,0},{251,1},{252,2},{253,3},{254,4},{255,5},{240,6},{241,7},{2... | collective-permute-start | bytes 516104 | tf_op jit(solution)/shard_map/while/body/eval_jaxpr/cond/branch_2_fun/cond/branch_2_fun/ppermute | solution.py:417
  22.9 11.2 %collective-permute-start.21 = (f32[168,256]{1,0:T(8,128)S(1)}, f32[168,256]{1,0:T(8,128)}, u32[]{:S(2)}, u32[]{:S(2)}) collective-permute-start(f32[168,256]{1,0:T(8,128)S(1)} %get-tuple-element.498), channel_id=1, source_target_pairs={{22,0},{23,1},{24,2},{25,3},{26,4},{27,5},{28,6},{29,7},{30,8},{31... | collective-permute-start | bytes 516104 | tf_op jit(solution)/shard_map/while/body/eval_jaxpr/cond/branch_2_fun/cond/branch_2_fun/ppermute | solution.py:417
  40.5 12.5 %collective-permute-start.32 = (f32[208,256]{1,0:T(8,128)S(1)}, f32[208,256]{1,0:T(8,128)S(1)}, u32[]{:S(2)}, u32[]{:S(2)}) collective-permute-start(f32[208,256]{1,0:T(8,128)S(1)} %get-tuple-element.515), channel_id=1, source_target_pairs={{15,0},{0,1},{1,2},{2,3},{3,4},{4,5},{5,6},{6,7},{7,8},{8,9},{9,10... | collective-permute-start | bytes 638984 | tf_op jit(solution)/shard_map/while/body/eval_jaxpr/cond/branch_1_fun/ppermute | solution.py:410
  43.5 9.6 %collective-permute-start.33 = (f32[208,256]{1,0:T(8,128)S(1)}, f32[208,256]{1,0:T(8,128)S(1)}, u32[]{:S(2)}, u32[]{:S(2)}) collective-permute-start(f32[208,256]{1,0:T(8,128)S(1)} %get-tuple-element.516), channel_id=1, source_target_pairs={{1,0},{2,1},{3,2},{4,3},{5,4},{6,5},{7,6},{8,7},{9,8},{10,9},{11,1... | collective-permute-start | bytes 638984 | tf_op jit(solution)/shard_map/while/body/eval_jaxpr/cond/branch_1_fun/ppermute | solution.py:410
  43.5 9.6 %collective-permute-start.34 = (f32[8,256]{1,0:T(8,128)S(1)}, f32[8,256]{1,0:T(8,128)}, u32[]{:S(2)}, u32[]{:S(2)}) collective-permute-start(f32[8,256]{1,0:T(8,128)S(1)} %get-tuple-element.783), channel_id=1, source_target_pairs={{0,64},{16,80},{32,96},{48,112},{64,128},{80,144},{96,160},{112,17... | collective-permute-start | bytes 24584 | tf_op jit(solution)/shard_map/while/body/eval_jaxpr/cond/branch_1_fun/ppermute | solution.py:480
  44.3 8.8 %collective-permute-start.35 = (f32[8,256]{1,0:T(8,128)S(1)}, f32[8,256]{1,0:T(8,128)}, u32[]{:S(2)}, u32[]{:S(2)}) collective-permute-start(f32[8,256]{1,0:T(8,128)S(1)} %get-tuple-element.783), channel_id=1, source_target_pairs={{0,128},{16,144},{32,160},{48,176},{64,192},{80,208},{96,224},{112... | collective-permute-start | bytes 24584 | tf_op jit(solution)/shard_map/while/body/eval_jaxpr/cond/branch_1_fun/ppermute | solution.py:480
  49.4 4.4 %collective-permute-start.36 = (f32[8,256]{1,0:T(8,128)S(1)}, f32[8,256]{1,0:T(8,128)}, u32[]{:S(2)}, u32[]{:S(2)}) collective-permute-start(f32[8,256]{1,0:T(8,128)S(1)} %get-tuple-element.783), channel_id=1, source_target_pairs={{0,192},{16,208},{32,224},{48,240},{64,0},{80,16},{96,32},{112,48}... | collective-permute-start | bytes 24584 | tf_op jit(solution)/shard_map/while/body/eval_jaxpr/cond/branch_1_fun/ppermute | solution.py:480
  55.0 14.9 %collective-permute-start.30 = (f32[168,256]{1,0:T(8,128)S(1)}, f32[168,256]{1,0:T(8,128)}, u32[]{:S(2)}, u32[]{:S(2)}) collective-permute-start(f32[168,256]{1,0:T(8,128)S(1)} %get-tuple-element.510), channel_id=1, source_target_pairs={{255,0},{240,1},{241,2},{242,3},{243,4},{244,5},{245,6},{246,7},{2... | collective-permute-start | bytes 516104 | tf_op jit(solution)/shard_map/while/body/eval_jaxpr/cond/branch_3_fun/cond/branch_3_fun/ppermute | solution.py:417
  59.5 18.0 %collective-permute-start.31 = (f32[168,256]{1,0:T(8,128)S(1)}, f32[168,256]{1,0:T(8,128)}, u32[]{:S(2)}, u32[]{:S(2)}) collective-permute-start(f32[168,256]{1,0:T(8,128)S(1)} %get-tuple-element.511), channel_id=1, source_target_pairs={{17,0},{18,1},{19,2},{20,3},{21,4},{22,5},{23,6},{24,7},{25,8},{26... | collective-permute-start | bytes 516104 | tf_op jit(solution)/shard_map/while/body/eval_jaxpr/cond/branch_3_fun/cond/branch_3_fun/ppermute | solution.py:417
